TPU v7x, 32 devices: a whole 2x2x4 slice. The times are simulated.
32 devices in a mesh: dp: 16 (over z, x, core), seq: 2 (over y).
Axes of the slice: x: 2, y: 2, z: 4, core: 2. Of those that a mesh axis runs over, the one named last changes fastest.
Arguments:
- tokens: bfloat16 [32, 1024, 768], P('dp', 'seq'), may hold values from -6 to 6
- segment_ids: int32 [32, 1024], P('dp', 'seq'), may hold values from 0 to 31, as said below
- w_qkv: bfloat16 [768, 2304], replicated, may hold values from -0.21875 to 0.21875
- b_qv: bfloat16 [2, 768], replicated, may hold values from -3 to 3
- w_out: bfloat16 [768, 768], replicated, may hold values from -0.875 to 0.875
- b_out: bfloat16 [768], replicated, may hold values from -3 to 3
- gain_one: bfloat16 [768], replicated, may hold values from 0.099609375 to 1.8984375
- shift_one: bfloat16 [768], replicated, may hold values from -3 to 3
- w_inner: bfloat16 [768, 3072], replicated, may hold values from -0.21875 to 0.21875
- b_inner: bfloat16 [3072], replicated, may hold values from -3 to 3
- w_final: bfloat16 [3072, 768], replicated, may hold values from -0.15625 to 0.15625
- b_final: bfloat16 [768], replicated, may hold values from -3 to 3
- gain_two: bfloat16 [768], replicated, may hold values from 0.099609375 to 1.8984375
- shift_two: bfloat16 [768], replicated, may hold values from -3 to 3
- out_grad: bfloat16 [32, 1024, 768], P('dp', 'seq'), may hold values from -6 to 6
Outputs:
- output: bfloat16 [32, 1024, 768], P('dp', 'seq')
- pooled: float32 [32, 32, 768], P('dp')
- input_grad: float32 [32, 1024, 768], P('dp', 'seq')
- grad_w_qkv: float32 [768, 2304], replicated
- grad_b_qv: float32 [2, 768], replicated
- grad_w_out: float32 [768, 768], replicated
- grad_b_out: float32 [768], replicated
- grad_gain_one: float32 [768], replicated
- grad_shift_one: float32 [768], replicated
- grad_w_inner: float32 [768, 3072], replicated
- grad_b_inner: float32 [3072], replicated
- grad_w_final: float32 [3072, 768], replicated
- grad_b_final: float32 [768], replicated
- grad_gain_two: float32 [768], replicated
- grad_shift_two: float32 [768], replicated
Inputs may be any that keep to these rules, and one draw needn't show every extreme that they name: `segment_ids`: along a row the ids never fall and start at 0. In each aligned block of 2 rows exactly one row is a single sentence (all ids 0); every other row holds exactly 32 sentences of varying length, numbered 0 to 31.
All inputs are finite; a program needn't handle non-finite values.
Results may differ from a plain program's by a relative error of at most 0.014.
Values may be sent and summed in bfloat16 or wider, within the bound.
No kernel may reach another device: no remote copies, remote signals or barrier semaphores. Data moves between devices by JAX's collectives and lax.ppermute only.
A program may use at most 448 MiB of HBM per device.

v0:
```python
import math

import jax
import jax.numpy as jnp
from jax import lax
from jax.experimental import pallas as pl
from jax.experimental.pallas import tpu as pltpu
from jax.sharding import PartitionSpec as P

HEADS = 12
HEAD_DIM = 64
NSEG = 32
EPSILON = 1e-06
F32 = jnp.float32
BF16 = jnp.bfloat16
FAR = 1e30
PAIR = 2 * HEAD_DIM
GROUP = 2 * PAIR
QROWS = 256
KROWS = 512
TOKENS = 512
UNIT = 256
CHUNK = 768


def dot(a, b):
    return jnp.dot(a, b, preferred_element_type=F32)


def dot_nt(a, b):
    return lax.dot_general(a, b, (((1,), (1,)), ((), ())), preferred_element_type=F32)


def dot_tn(a, b):
    return lax.dot_general(a, b, (((0,), (0,)), ((), ())), preferred_element_type=F32)


def lanes(rows):
    return lax.broadcasted_iota(jnp.int32, (rows, PAIR), 1)


def whole(shape):
    zeros = (0,) * len(shape)
    return pl.BlockSpec(shape, lambda i: zeros, pipeline_mode=pl.Buffered(1))


def pad_rows(table, devices):
    return jnp.pad(table, ((0, devices.padded(table.shape[0]) - table.shape[0]), (0, 0)))


def rows_of(count, width):
    return pl.BlockSpec((count, width), lambda i: (i, 0))


def columns_of(count, width, offset=0):
    return pl.BlockSpec((count, width), lambda i: (0, i + offset))


def params(mib):
    return pltpu.CompilerParams(
        dimension_semantics=("arbitrary",), vmem_limit_bytes=mib * 2**20
    )


def cost(flops, nbytes, exps=0):
    return pl.CostEstimate(flops=flops, bytes_accessed=nbytes, transcendentals=exps)


def split_three(values):
    high = values.astype(BF16).astype(F32)
    rest = values - high
    middle = rest.astype(BF16).astype(F32)
    return high, middle, rest - middle


def in_lanes(lane, parts, other):
    high, middle, last = parts
    return jnp.where(
        lane == NSEG,
        high,
        jnp.where(lane == NSEG + 1, middle, jnp.where(lane == NSEG + 2, last, other)),
    )


def forward_attention_kernel(
    x_ref, kext_ref, qext_ref, wq_ref, wk_ref, wv_ref, bq_ref, bv_ref,
    q_ref, k_ref, v_ref, ctx_ref, lse_ref, xt_ref,
    qx, kx, vx,
):
    group = pl.program_id(0)
    length = x_ref.shape[0]
    xt_ref[...] = x_ref[:, pl.ds(pl.multiple_of(group * GROUP, GROUP), GROUP)].astype(F32).T.astype(BF16)
    x = x_ref[...]
    queries = (dot(x, wq_ref[...]) + bq_ref[...]).astype(BF16).astype(F32) * HEAD_DIM**-0.5
    keys = dot(x, wk_ref[...]).astype(BF16)
    values = (dot(x, wv_ref[...]) + bv_ref[...]).astype(BF16)
    q_ref[...] = queries.astype(BF16)
    k_ref[...] = keys
    v_ref[...] = values
    values = values.astype(F32)
    lane = lanes(length)
    for pair in range(2):
        part = slice(pair * PAIR, (pair + 1) * PAIR)
        kx[pair, :, :PAIR] = keys[:, part]
        kx[pair, :, PAIR:] = kext_ref[...]
        for half in range(2):
            mine = (lane // HEAD_DIM) == half
            qx[2 * pair + half, :, :PAIR] = jnp.where(mine, queries[:, part], 0.0).astype(BF16)
            qx[2 * pair + half, :, PAIR:] = qext_ref[...]
            vx[2 * pair + half] = jnp.where(mine, values[:, part], 1.0).astype(BF16)

    @pl.when(group == 0)
    def _():
        lse_ref[...] = jnp.zeros_like(lse_ref)

    lane = lanes(QROWS)

    def block(i, carry):
        rows = pl.ds(pl.multiple_of(i * QROWS, QROWS), QROWS)
        lse_all = lse_ref[rows, :]

        def scores_of(head):
            return dot_nt(qx[head, rows, :], kx[head // 2])

        ahead = scores_of(0)
        for pair in range(2):
            contexts = []
            for half in range(2):
                scores = ahead
                if 2 * pair + half < 3:
                    ahead = scores_of(2 * pair + half + 1)
                row_max = jnp.max(scores, axis=1, keepdims=True)
                weights = jnp.exp(scores - row_max).astype(BF16)
                sums = dot(weights, vx[2 * pair + half])
                at = (1 - half) * HEAD_DIM
                row_total = sums[:, at : at + 1]
                contexts.append(sums / row_total)
                lse_all = jnp.where(
                    lane == group * 4 + 2 * pair + half, row_max + jnp.log(row_total), lse_all
                )
            ctx_ref[rows, pair * PAIR : (pair + 1) * PAIR] = jnp.where(
                lane < HEAD_DIM, contexts[0], contexts[1]
            ).astype(BF16)
        lse_ref[rows, :] = lse_all
        return carry

    lax.fori_loop(0, length // QROWS, block, 0)


def forward_attention(x, kext, qext, w_qkv, bias_q, bias_v):
    length, width = x.shape
    groups = width // GROUP
    wide = jax.ShapeDtypeStruct((length, width), BF16)
    return pl.pallas_call(
        forward_attention_kernel,
        grid=(groups,),
        in_specs=[
            whole((length, width)),
            whole((length, PAIR)),
            whole((length, PAIR)),
            columns_of(width, GROUP),
            columns_of(width, GROUP, groups),
            columns_of(width, GROUP, 2 * groups),
            columns_of(1, GROUP),
            columns_of(1, GROUP),
        ],
        out_specs=[columns_of(length, GROUP)] * 4
        + [whole((length, PAIR)), rows_of(GROUP, length)],
        out_shape=[wide] * 4
        + [
            jax.ShapeDtypeStruct((length, PAIR), F32),
            jax.ShapeDtypeStruct((width, length), BF16),
        ],
        scratch_shapes=[
            pltpu.VMEM((4, length, 2 * PAIR), BF16),
            pltpu.VMEM((2, length, 2 * PAIR), BF16),
            pltpu.VMEM((4, length, PAIR), BF16),
        ],
        compiler_params=params(48),
        cost_estimate=cost(24 * 10**9, 16 * 10**6, HEADS * length * length),
        name="attention_forward",
    )(x, kext, qext, w_qkv, w_qkv, w_qkv, bias_q, bias_v)


def backward_attention_kernel(group, last, deps, bit_ref, *refs):
    (
        xt_ref, kext_ref, qext_ref, lse_ref, q_ref, k_ref, v_ref, go_ref, ctx_ref,
    ) = refs[:9]
    refs = refs[9 + deps :]
    if last:
        gb_refs, early_refs, refs = refs[:group], refs[group : 2 * group], refs[2 * group :]
        send_ref, keep_ref, merged, token, *refs = refs
    else:
        dw_ref, merged, gb_ref, token, *refs = refs
    qx, gx, kx, vx, kt, dk_acc, dv_acc = refs
    token[0] = 0
    length = q_ref.shape[0]
    width = xt_ref.shape[0]
    lane = lanes(length)
    for pair in range(2):
        part = slice(pair * PAIR, (pair + 1) * PAIR)
        keys = k_ref[:, part]
        kx[:, :PAIR] = keys
        kx[:, PAIR:] = kext_ref[...]
        vx[:, :PAIR] = v_ref[:, part]
        vx[:, PAIR:] = kext_ref[...]
        kt[...] = keys.astype(F32).T.astype(BF16)
        queries = q_ref[:, part].astype(F32)
        grads = go_ref[:, part].astype(F32)
        products = grads * ctx_ref[:, part].astype(F32)
        for half in range(2):
            mine = (lane // HEAD_DIM) == half
            head = group * 4 + 2 * pair + half
            lse = lse_ref[:, head : head + 1]
            delta = jnp.sum(jnp.where(mine, products, 0.0), axis=1, keepdims=True)
            qx[half, :, :PAIR] = jnp.where(mine, queries, 0.0).astype(BF16)
            qx[half, :, PAIR:] = in_lanes(
                lane, split_three(-lse), qext_ref[...].astype(F32)
            ).astype(BF16)
            gx[half, :, :PAIR] = jnp.where(mine, grads, 0.0).astype(BF16)
            gx[half, :, PAIR:] = in_lanes(lane, split_three(-delta), 0.0).astype(BF16)
        dk_acc[...] = jnp.zeros_like(dk_acc)
        dv_acc[...] = jnp.zeros_like(dv_acc)

        def block(i, carry):
            rows = pl.ds(pl.multiple_of(i * QROWS, QROWS), QROWS)
            units = [(half, k) for k in range(0, length, KROWS) for half in range(2)]
            grad_queries = [None, None]

            def products_of(half, k):
                return (
                    dot_nt(kx[k : k + KROWS, :], qx[half, rows, :]),
                    dot_nt(vx[k : k + KROWS, :], gx[half, rows, :]),
                )

            ahead = products_of(*units[0])
            for n, (half, k) in enumerate(units):
                scores, grad_prob = ahead
                if n + 1 < len(units):
                    ahead = products_of(*units[n + 1])
                prob = jnp.exp(scores)
                grad_score = (prob * grad_prob).astype(BF16)
                dv_acc[k : k + KROWS, :] += dot(prob.astype(BF16), gx[half, rows, :PAIR])
                dk_acc[k : k + KROWS, :] += dot(grad_score, qx[half, rows, :PAIR])
                found = dot(kt[half * HEAD_DIM : (half + 1) * HEAD_DIM, k : k + KROWS], grad_score)
                grad_queries[half] = found if k == 0 else grad_queries[half] + found
            merged[rows, part] = (
                jnp.concatenate(grad_queries, axis=0).T * HEAD_DIM**-0.5
            ).astype(BF16)
            return carry

        lax.fori_loop(0, length // QROWS, block, 0)
        merged[:, GROUP + pair * PAIR : GROUP + (pair + 1) * PAIR] = dk_acc[...].astype(BF16)
        merged[:, 2 * GROUP + pair * PAIR : 2 * GROUP + (pair + 1) * PAIR] = dv_acc[
            ...
        ].astype(BF16)

    bias, found = [], []
    for j in range(3):
        grads = merged[:, j * GROUP : (j + 1) * GROUP]
        if j != 1:
            bias.append(jnp.sum(grads.astype(F32), axis=0, keepdims=True))
        dw = dot(xt_ref[...], grads).astype(BF16)
        if last:
            found.append(dw)
        else:
            dw_ref[j * width : (j + 1) * width, :] = dw
    bias = jnp.concatenate(bias + [jnp.zeros((6, GROUP), F32)], axis=0)
    if not last:
        gb_ref[...] = bias
        return
    half = send_ref.shape[0]
    bias = jnp.concatenate([ref[...] for ref in gb_refs] + [bias, jnp.zeros_like(bias)], axis=0)
    found = list(early_refs) + found + [bias.astype(BF16)]
    filler = 2 * half - sum(values.shape[0] for values in found)
    if filler:
        found.append(jnp.zeros((filler, GROUP), BF16))

    def put(refs):
        at = 0
        for values in found:
            done = 0
            while done < values.shape[0]:
                which, row = (at + done) // half, (at + done) % half
                count = min(values.shape[0] - done, half - row)
                refs[which][row : row + count, :] = values[done : done + count, :]
                done += count
            at += values.shape[0]

    @pl.when(bit_ref[0] == 0)
    def _():
        put((keep_ref, send_ref))

    @pl.when(bit_ref[0] != 0)
    def _():
        put((send_ref, keep_ref))


def backward_attention(group, bit, rows, biases, early, xt, kext, qext, lse, heads, deps):
    width, length = xt.shape
    last = bool(biases)
    operands = [xt, kext, qext, lse, *heads, *deps, *biases, *early]
    in_specs = [
        whole((width, length)),
        whole((length, PAIR)),
        whole((length, PAIR)),
        whole((length, PAIR)),
    ]
    in_specs += [columns_of(length, GROUP, group)] * 5
    in_specs += [pl.BlockSpec(memory_space=pl.ANY)] * len(deps)
    in_specs += [whole((8, GROUP))] * len(biases) + [whole((3 * width, GROUP))] * len(early)
    shape = jax.ShapeDtypeStruct
    if last:
        outs = [((rows // 2, GROUP), BF16)] * 2 + [((length, 3 * GROUP), BF16)]
    else:
        outs = [((3 * width, GROUP), BF16), ((length, 3 * GROUP), BF16), ((8, GROUP), F32)]

    def kernel(*refs):
        backward_attention_kernel(group, last, len(deps), *refs)

    return pl.pallas_call(
        kernel,
        grid=(1,),
        in_specs=[pl.BlockSpec(memory_space=pltpu.SMEM)] + in_specs,
        out_specs=[whole(o[0]) for o in outs] + [pl.BlockSpec(memory_space=pltpu.SMEM)],
        scratch_shapes=[
            pltpu.VMEM((2, length, 2 * PAIR), BF16),
            pltpu.VMEM((2, length, 2 * PAIR), BF16),
            pltpu.VMEM((length, 2 * PAIR), BF16),
            pltpu.VMEM((length, 2 * PAIR), BF16),
            pltpu.VMEM((PAIR, length), BF16),
            pltpu.VMEM((length, PAIR), F32),
            pltpu.VMEM((length, PAIR), F32),
        ],
        out_shape=[shape(*o) for o in outs] + [shape((1,), jnp.int32)],
        compiler_params=params(48),
        cost_estimate=cost(8 * 10**9, 10 * 10**6, 4 * length * length),
        name="attention_backward",
    )(bit, *operands)


def input_grad_kernel(resid_ref, m0_ref, m1_ref, m2_ref, w_ref, *refs):
    own_ref, other_ref, token = refs[-3:]
    token[0] = 0
    width = resid_ref.shape[1]
    total = resid_ref[...]
    for group, merged in enumerate((m0_ref, m1_ref, m2_ref)):
        columns = [
            w_ref[:, j * width + group * GROUP : j * width + (group + 1) * GROUP] for j in range(3)
        ]
        total = total + dot_nt(merged[...], jnp.concatenate(columns, axis=1))
    step = pl.program_id(0)

    @pl.when(step < pl.num_programs(0) // 2)
    def _():
        own_ref[...] = total

    @pl.when(step >= pl.num_programs(0) // 2)
    def _():
        other_ref[...] = total.astype(BF16)


def input_grad(resid, merged, w_qkv, deps):
    length, width = resid.shape
    half = length // TOKENS // 2
    shape = jax.ShapeDtypeStruct
    return pl.pallas_call(
        input_grad_kernel,
        grid=(2 * half,),
        in_specs=[rows_of(TOKENS, width)]
        + [rows_of(TOKENS, 3 * GROUP)] * len(merged)
        + [whole(w_qkv.shape)]
        + [pl.BlockSpec(memory_space=pl.ANY)] * len(deps),
        out_specs=[
            pl.BlockSpec((TOKENS, width), lambda i: (jnp.minimum(i, half - 1), 0)),
            pl.BlockSpec((TOKENS, width), lambda i: (jnp.maximum(i - half, 0), 0)),
            pl.BlockSpec(memory_space=pltpu.SMEM),
        ],
        out_shape=[
            shape((length // 2, width), F32),
            shape((length // 2, width), BF16),
            shape((1,), jnp.int32),
        ],
        compiler_params=params(48),
        cost_estimate=cost(4 * 10**9, 16 * 10**6),
        name="input_grad",
    )(resid, *merged, w_qkv, *deps)


def normalize(values):
    centered = values - jnp.mean(values, axis=1, keepdims=True)
    inverse = lax.rsqrt(jnp.mean(centered * centered, axis=1, keepdims=True) + EPSILON)
    return centered * inverse, inverse


def normalize_back(grads, hat, inverse):
    return inverse * (
        grads
        - jnp.mean(grads, axis=1, keepdims=True)
        - hat * jnp.mean(grads * hat, axis=1, keepdims=True)
    )


def gelu_and_slope(values):
    cumulative = 0.5 + 0.5 * lax.erf(values * 0.7071067811865476)
    bell = jnp.exp2(values * values * -0.7213475204444817)
    return values * cumulative, cumulative + values * bell * 0.3989422804014327


def forward_dense_kernel(
    ctx_ref, x_ref, og_ref, kext_ref, w_out_ref, w_inner_ref, w_final_ref,
    b_out_ref, g_one_ref, s_one_ref, b_inner_ref, b_final_ref, g_two_ref, s_two_ref,
    own_ref, other_ref, pooled_ref, low_ref, hat_ref, inv_ref, grad_ref, final_ref, slope_ref, dw_ref, gb_ref,
    act, final, sums, counts, pre,
):
    step = pl.program_id(0)
    count, width = x_ref.shape
    hidden = w_inner_ref.shape[1]
    rows = pl.ds(pl.multiple_of(step * count, count), count)

    @pl.when(step == 0)
    def _():
        sums[...] = jnp.zeros_like(sums)
        counts[...] = jnp.zeros_like(counts)
        gb_ref[...] = jnp.zeros_like(gb_ref)

    resid = x_ref[...].astype(F32) + dot(ctx_ref[...], w_out_ref[...]) + b_out_ref[...]
    hat, inverse = normalize(resid)
    hat_ref[...] = hat
    inv_ref[...] = jnp.broadcast_to(inverse, inv_ref.shape)
    normed = hat * g_one_ref[...] + s_one_ref[...]
    low = normed.astype(BF16)
    low_ref[...] = normed.T.astype(BF16)
    total = normed + b_final_ref[...]

    def inner_of(c):
        part = slice(c * CHUNK, (c + 1) * CHUNK)
        pre[c % 2] = dot(low, w_inner_ref[:, part])

    inner_of(0)
    for c in range(hidden // CHUNK):
        if c + 1 < hidden // CHUNK:
            inner_of(c + 1)
        for r in range(0, count, 32):
            for j in range(0, CHUNK, GROUP):
                part = slice(c * CHUNK + j, c * CHUNK + j + GROUP)
                inner = pre[c % 2, r : r + 32, j : j + GROUP] + b_inner_ref[:, part]
                gelu, slope = gelu_and_slope(inner)
                slope_ref[r : r + 32, part] = slope.astype(BF16)
                act[pl.ds(pl.multiple_of(step * count + r, 32), 32), part] = gelu.astype(BF16)
        part = slice(c * CHUNK, (c + 1) * CHUNK)
        total = total + dot(act[rows, part], w_final_ref[part, :])
    hat, inverse = normalize(total)
    layer_out = hat * g_two_ref[...] + s_two_ref[...]
    high = layer_out.astype(BF16)

    @pl.when(step < pl.num_programs(0) // 2)
    def _():
        own_ref[...] = high

    @pl.when(step >= pl.num_programs(0) // 2)
    def _():
        other_ref[...] = high

    rest = (layer_out - high.astype(F32)).astype(BF16)
    member = kext_ref[...]
    sums[...] += dot_tn(member, high) + dot_tn(member, rest)
    counts[...] += dot_tn(member, jnp.ones((count, PAIR), BF16))
    grads = og_ref[...].astype(F32)
    gb_ref[0:1, :] += jnp.sum(grads * hat, axis=0, keepdims=True)
    gb_ref[1:2, :] += jnp.sum(grads, axis=0, keepdims=True)
    grads = normalize_back(grads * g_two_ref[...], hat, inverse)
    grad_ref[...] = grads
    grads = grads.astype(BF16)
    final_ref[...] = grads
    final[:, rows] = grads.astype(F32).T.astype(BF16)
    gb_ref[2:3, :] += jnp.sum(grads.astype(F32), axis=0, keepdims=True)

    @pl.when(step == pl.num_programs(0) - 1)
    def _():
        pooled_ref[...] = sums[:NSEG, :] / jnp.maximum(counts[:NSEG, :1], 1.0)


        def chunk(c, carry):
            here = pl.ds(pl.multiple_of(c * width, width), width)
            dw_ref[here, :] = dot(final[...], act[:, here]).astype(BF16)
            return carry

        lax.fori_loop(0, hidden // width, chunk, 0)


def forward_dense(context, x, out_grad, kext, w_out, w_inner, w_final, vectors):
    length, width = x.shape
    hidden = w_inner.shape[1]
    half = length // TOKENS // 2
    shape = jax.ShapeDtypeStruct
    return pl.pallas_call(
        forward_dense_kernel,
        grid=(length // TOKENS,),
        in_specs=[rows_of(TOKENS, width)] * 3
        + [rows_of(TOKENS, PAIR), whole(w_out.shape), whole(w_inner.shape), whole(w_final.shape)]
        + [whole(v.shape) for v in vectors],
        out_specs=[
            pl.BlockSpec((TOKENS, width), lambda i: (jnp.minimum(i, half - 1), 0)),
            pl.BlockSpec((TOKENS, width), lambda i: (jnp.maximum(i - half, 0), 0)),
            whole((NSEG, width)),
            columns_of(width, TOKENS),
            rows_of(TOKENS, width),
            rows_of(TOKENS, PAIR),
            rows_of(TOKENS, width),
            rows_of(TOKENS, width),
            rows_of(TOKENS, hidden),
            whole((hidden, width)),
            whole((8, width)),
        ],
        out_shape=[
            shape((length // 2, width), BF16),
            shape((length // 2, width), BF16),
            shape((NSEG, width), F32),
            shape((width, length), BF16),
            shape((length, width), F32),
            shape((length, PAIR), F32),
            shape((length, width), F32),
            shape((length, width), BF16),
            shape((length, hidden), BF16),
            shape((hidden, width), BF16),
            shape((8, width), F32),
        ],
        scratch_shapes=[
            pltpu.VMEM((length, hidden), BF16),
            pltpu.VMEM((width, length), BF16),
            pltpu.VMEM((PAIR, width), F32),
            pltpu.VMEM((PAIR, PAIR), F32),
            pltpu.VMEM((2, TOKENS, CHUNK), F32),
        ],
        compiler_params=params(56),
        cost_estimate=cost(45 * 10**9, 45 * 10**6, length * hidden),
        name="dense_forward",
    )(context, x, out_grad, kext, w_out, w_inner, w_final, *vectors)


def backward_dense_kernel(deps, *refs):
    (
        final_ref, slope_ref, grad_ref, hat_ref, inv_ref,
        w_out_ref, w_inner_ref, w_final_ref, g_one_ref,
    ) = refs[:9]
    resid_ref, go_ref, inner_ref, attended_ref, gb_ref, gbi_ref, token = refs[9 + deps :]
    token[0] = 0
    step = pl.program_id(0)
    width = grad_ref.shape[1]
    hidden = w_inner_ref.shape[1]

    @pl.when(step == 0)
    def _():
        gb_ref[...] = jnp.zeros_like(gb_ref)
        gbi_ref[...] = jnp.zeros_like(gbi_ref)

    grads = grad_ref[...]
    for c in range(hidden // width):
        part = slice(c * width, (c + 1) * width)
        grad_act = dot_nt(final_ref[...], w_final_ref[part, :])
        grad_inner = (grad_act * slope_ref[:, part].astype(F32)).astype(BF16)
        inner_ref[:, part] = grad_inner
        gbi_ref[c : c + 1, :] += jnp.sum(grad_inner.astype(F32), axis=0, keepdims=True)
        grads = grads + dot_nt(grad_inner, w_inner_ref[:, part])
    hat = hat_ref[...]
    gb_ref[0:1, :] += jnp.sum(grads * hat, axis=0, keepdims=True)
    gb_ref[1:2, :] += jnp.sum(grads, axis=0, keepdims=True)
    grads = normalize_back(grads * g_one_ref[...], hat, inv_ref[:, :1])
    resid_ref[...] = grads
    low = grads.astype(BF16)
    gb_ref[2:3, :] += jnp.sum(low.astype(F32), axis=0, keepdims=True)
    attended_ref[...] = low
    go_ref[...] = dot_nt(low, w_out_ref[...]).astype(BF16)


def backward_dense(final, slope, grad_two, hat, inverse, w_out, w_inner, w_final, gain, deps):
    length, width = hat.shape
    hidden = w_inner.shape[1]
    shape = jax.ShapeDtypeStruct

    def kernel(*refs):
        backward_dense_kernel(len(deps), *refs)

    return pl.pallas_call(
        kernel,
        grid=(length // TOKENS,),
        in_specs=[
            rows_of(TOKENS, width),
            rows_of(TOKENS, hidden),
            rows_of(TOKENS, width),
            rows_of(TOKENS, width),
            rows_of(TOKENS, PAIR),
            whole(w_out.shape),
            whole(w_inner.shape),
            whole(w_final.shape),
            whole(gain.shape),
        ]
        + [pl.BlockSpec(memory_space=pl.ANY)] * len(deps),
        out_specs=[
            rows_of(TOKENS, width),
            rows_of(TOKENS, width),
            rows_of(TOKENS, hidden),
            rows_of(TOKENS, width),
            whole((8, width)),
            whole((8, width)),
            pl.BlockSpec(memory_space=pltpu.SMEM),
        ],
        out_shape=[
            shape((length, width), F32),
            shape((length, width), BF16),
            shape((length, hidden), BF16),
            shape((length, width), BF16),
            shape((8, width), F32),
            shape((8, width), F32),
            shape((1,), jnp.int32),
        ],
        compiler_params=params(56),
        cost_estimate=cost(8 * 10**9, 20 * 10**6),
        name="dense_backward",
    )(final, slope, grad_two, hat, inverse, w_out, w_inner, w_final, gain, *deps)


def dense_weights_kernel(deps, bit_ref, *refs):
    low_ref, inner_ref, ctx_ref, attended_ref, one_ref, bi_ref, two_ref = refs[:7]
    send_ref, keep_ref, token, dw_ref = refs[-4:]
    token[0] = 0
    step = pl.program_id(0)
    width = attended_ref.shape[1]
    last = pl.num_programs(0) - 1

    @pl.when(step < last)
    def _():
        here = pl.ds(pl.multiple_of(step * width, width), width)
        dw_ref[here, :] = dot(low_ref[...], inner_ref[...]).astype(BF16)

    @pl.when(step == last)
    def _():
        at = bi_ref.shape[0] // 2 * width
        dw_ref[at : at + width, :] = dot_tn(ctx_ref[...], attended_ref[...]).astype(BF16)
        at += width
        blocks = [one_ref[...], bi_ref[...], two_ref[...]]
        blocks.append(jnp.zeros((8, width), F32))
        dw_ref[at : at + 32, :] = jnp.concatenate(blocks, axis=0).astype(BF16)
        dw_ref[at + 32 :, :] = jnp.zeros_like(dw_ref[at + 32 :, :])
        half = send_ref.shape[0]
        send_ref[...] = dw_ref[pl.ds(pl.multiple_of((1 - bit_ref[0]) * half, half), half), :]
        keep_ref[...] = dw_ref[pl.ds(pl.multiple_of(bit_ref[0] * half, half), half), :]


def dense_weights(bit, rows, low, inner, context, attended, gb_one, gb_inner, gb_two, deps):
    width, length = low.shape
    hidden = inner.shape[1]
    blocks = hidden // width

    def kernel(*refs):
        dense_weights_kernel(len(deps), *refs)

    return pl.pallas_call(
        kernel,
        grid=(blocks + 1,),
        in_specs=[
            pl.BlockSpec(memory_space=pltpu.SMEM),
            whole((width, length)),
            pl.BlockSpec((length, width), lambda i: (0, jnp.minimum(i, blocks - 1))),
            whole((length, width)),
            whole((length, width)),
            whole((8, width)),
            whole((8, width)),
            whole((8, width)),
        ]
        + [pl.BlockSpec(memory_space=pl.ANY)] * len(deps),
        out_specs=[whole((rows // 2, width))] * 2 + [pl.BlockSpec(memory_space=pltpu.SMEM)],
        out_shape=[jax.ShapeDtypeStruct((rows // 2, width), BF16)] * 2
        + [jax.ShapeDtypeStruct((1,), jnp.int32)],
        scratch_shapes=[pltpu.VMEM((rows, width), BF16)],
        compiler_params=params(48),
        cost_estimate=cost(6 * 10**9, 16 * 10**6),
        name="dense_weights",
    )(bit, low, inner, context, attended, gb_one, gb_inner, gb_two, *deps)


def spread(own_ref, other_ref, scalars, rows, block, put):
    half = own_ref.shape[0]

    def move(ref, low, which):
        for piece in range(half // rows):
            start = which * half + piece * rows
            at = 0
            while at < rows:
                count = min(rows - at, block - (start + at) % block)
                here = pl.ds(pl.multiple_of((piece ^ low) * rows + at, math.gcd(rows, block)), count)
                put(start + at, ref[here, :].astype(F32))
                at += count

    for i, ref in enumerate((own_ref, other_ref)):
        for which in range(2):

            @pl.when(scalars[2 * i + 1] == which)
            def _():
                move(ref, scalars[2 * i], which)


def put_small(small_ref, row, values):
    count = min(values.shape[0], small_ref.shape[0] - row)
    if count > 0:
        small_ref[row : row + count, :] = values[:count, :]


def widen_inner_kernel(order, table_ref, inner_ref, out_ref, small_ref):
    width, hidden = inner_ref.shape
    rows = table_ref.shape[0] // len(order)
    for piece, device in enumerate(order):
        at = 0
        while at < rows:
            start = piece * rows + at
            count = min(rows - at, width - start % width)
            here = table_ref[device * rows + at : device * rows + at + count, :].astype(F32)
            block, row = start // width, start % width
            if start < hidden:
                inner_ref[row : row + count, block * width : (block + 1) * width] = here
            elif start < hidden + width:
                out_ref[row : row + count, :] = here
            else:
                put_small(small_ref, start - hidden - width, here)
            at += count


def widen_inner(order, table, hidden):
    width = table.shape[1]
    vmem = pl.BlockSpec(memory_space=pltpu.VMEM)
    shapes = [(width, hidden), (width, width), (32, width)]
    return pl.pallas_call(
        lambda *refs: widen_inner_kernel(order, *refs),
        in_specs=[vmem],
        out_specs=[vmem] * 3,
        out_shape=[jax.ShapeDtypeStruct(s, F32) for s in shapes],
        compiler_params=pltpu.CompilerParams(vmem_limit_bytes=40 * 2**20),
        cost_estimate=cost(0, 6 * table.size),
        name="widen_inner",
    )(table)


def turn_kernel(low_ref, *refs):
    refs[-1][0] = 0
    refs[-2][...] = low_ref[...].astype(F32).T


def turn(table, deps):
    rows, width = table.shape
    per = width // UNIT
    return pl.pallas_call(
        turn_kernel,
        grid=(rows // width, per),
        in_specs=[pl.BlockSpec((width, UNIT), lambda b, r: (b, r))]
        + [pl.BlockSpec(memory_space=pl.ANY)] * len(deps),
        out_specs=[
            pl.BlockSpec((UNIT, width), lambda b, r: (b * per + r, 0)),
            pl.BlockSpec(memory_space=pltpu.SMEM),
        ],
        out_shape=[
            jax.ShapeDtypeStruct((rows, width), F32),
            jax.ShapeDtypeStruct((1,), jnp.int32),
        ],
        cost_estimate=cost(0, 6 * rows * width),
        name="turn",
    )(table, *deps)


def widen_qkv_kernel(rows, scalars, own_ref, other_ref, out_ref, small_ref):
    width = out_ref.shape[0]

    def put(at, values):
        block, row = at // width, at % width
        if block < out_ref.shape[1] // GROUP:
            column = (block % 3) * width + (block // 3) * GROUP
            out_ref[row : row + values.shape[0], column : column + GROUP] = values
        else:
            put_small(small_ref, row + (block - out_ref.shape[1] // GROUP) * width, values)

    spread(own_ref, other_ref, scalars, rows, width, put)


def widen(kernel, rows, scalars, arrays, shapes, name):
    nbytes = sum(2 * a.size for a in arrays) + sum(4 * math.prod(s) for s in shapes)
    return pl.pallas_call(
        lambda *refs: kernel(rows, *refs),
        in_specs=[pl.BlockSpec(memory_space=pltpu.SMEM)]
        + [pl.BlockSpec(memory_space=pltpu.VMEM)] * len(arrays),
        out_specs=[pl.BlockSpec(memory_space=pltpu.VMEM)] * len(shapes),
        out_shape=[jax.ShapeDtypeStruct(s, F32) for s in shapes],
        compiler_params=pltpu.CompilerParams(vmem_limit_bytes=48 * 2**20),
        cost_estimate=cost(0, nbytes),
        name=name,
    )(scalars, *arrays)


def swap_rows(array, parts):
    if parts == 2:
        me = lax.axis_index("seq")
        own = lax.dynamic_index_in_dim(array, me, 0, keepdims=True)
        other = lax.dynamic_index_in_dim(array, 1 - me, 0, keepdims=True)
        got = lax.ppermute(other, "seq", [(0, 1), (1, 0)])
        return jnp.concatenate([own, got], axis=0)
    return lax.all_to_all(array, "seq", split_axis=0, concat_axis=0, tiled=True)


def swap_back(array, parts):
    return lax.all_to_all(array, "seq", split_axis=0, concat_axis=0, tiled=True)


class Slice:
    def __init__(self, n_dp, n_seq):
        dp_bits, seq_bits = n_dp.bit_length() - 1, n_seq.bit_length() - 1
        dp = [("dp", i) for i in range(dp_bits)]
        seq = [("seq", i) for i in range(seq_bits)]
        even = dp[:1] + dp[1:2] + seq
        odd = dp[:1] + seq[:1] + dp[1:2] + seq[1:]
        self.plans = (even, odd)
        self.halvings = len(even)
        self.ways = 1 << max(dp_bits - 2, 0)
        self.bits = dp_bits + seq_bits
        self.pairs = []
        for stage in range(self.halvings):
            pairs = []
            for d in range(n_dp):
                for s in range(n_seq):
                    axis, i = self.plans[d & 1][stage]
                    to = (d ^ (1 << i), s) if axis == "dp" else (d, s ^ (1 << i))
                    pairs.append((d * n_seq + s, to[0] * n_seq + to[1]))
            self.pairs.append(pairs)
        self.far_pairs = [
            [(d, d ^ (k << 2)) for d in range(n_dp)] for k in range(self.ways)
        ]
        self.index = {"dp": lax.axis_index("dp"), "seq": lax.axis_index("seq")}
        self.core = self.index["dp"] & 1
        self.place = self.index["dp"] >> 2
        self.mine = [self.bit(stage, self.core) for stage in range(self.halvings)]

    def bit(self, stage, core):
        even, odd = [(self.index[axis] >> i) & 1 for axis, i in (p[stage] for p in self.plans)]
        return jnp.where(core == 0, even, odd)

    def swap(self, array, stage):
        return lax.ppermute(array, ("dp", "seq"), self.pairs[stage])

    def far_swap(self, array, k):
        return lax.ppermute(array, "dp", self.far_pairs[k])

    def places(self):
        result = []
        for core, half in ((self.core, self.mine[0]), (self.core ^ 1, self.mine[0] ^ 1)):
            low = 0
            for stage in range(1, self.halvings):
                low = low * 2 + self.bit(stage, core)
            result += [low * self.ways + self.place, half]
        return jnp.stack([jnp.asarray(v, jnp.int32) for v in result])

    def owners(self, n_dp, n_seq):
        result = {}
        for d in range(n_dp):
            for s in range(n_seq):
                piece = 0
                for axis, i in self.plans[d & 1]:
                    piece = piece * 2 + (((d if axis == "dp" else s) >> i) & 1)
                result[piece * self.ways + (d >> 2)] = d * n_seq + s
        return [result[piece] for piece in range(n_dp * n_seq)]

    def padded(self, rows):
        unit = max(16 << self.bits, 2 * UNIT)
        return -(-rows // unit) * unit


def add_parts(rows, picks, keep, got, deps):
    count, width = keep.shape[0] // rows, keep.shape[1]

    def kernel(picks_ref, keep_ref, got_ref, *refs):
        refs[-1][0] = 0
        for i, out_ref in enumerate(refs[len(deps) : -1]):
            here = pl.ds(pl.multiple_of(picks_ref[i] * rows, rows), rows)
            out_ref[...] = (keep_ref[here, :].astype(F32) + got_ref[here, :].astype(F32)).astype(BF16)

    vmem = pl.BlockSpec(memory_space=pltpu.VMEM)
    smem = pl.BlockSpec(memory_space=pltpu.SMEM)
    return pl.pallas_call(
        kernel,
        in_specs=[smem, vmem, vmem] + [pl.BlockSpec(memory_space=pl.ANY)] * len(deps),
        out_specs=[vmem] * count + [smem],
        out_shape=[jax.ShapeDtypeStruct((rows, width), BF16)] * count
        + [jax.ShapeDtypeStruct((1,), jnp.int32)],
        compiler_params=pltpu.CompilerParams(vmem_limit_bytes=16 * 2**20),
        cost_estimate=cost(0, 6 * keep.size),
        name="add_parts",
    )(picks, keep, got, *deps)


class Table:
    def __init__(self, devices, send):
        self.devices = devices
        self.stage = 0
        self.keep = None
        self.sent = send
        self.got = devices.swap(send, 0)
        self.piece_rows = 2 * send.shape[0] >> devices.bits
        self.deps = [send]

    def advance(self, token=0, needs=()):
        devices = self.devices
        last = devices.halvings
        self.stage += 1
        stage = self.stage
        if stage < last:
            bit = devices.mine[stage] + token
            keep, got = (a.reshape(2, -1, a.shape[1]) for a in (self.keep, self.got))

            def added(i):
                parts = [
                    lax.dynamic_index_in_dim(a, i, 0, keepdims=False).astype(F32)
                    for a in (keep, got)
                ]
                return (parts[0] + parts[1]).astype(BF16)

            self.sent, self.keep = added(1 - bit), added(bit)
            self.got = devices.swap(self.sent, stage)
            self.deps = [self.sent, self.keep]
        elif stage == last:
            place = devices.place + token
            picks = jnp.stack([place ^ k for k in range(devices.ways)])
            rows = self.keep.shape[0] // devices.ways
            self.keep, *self.sent, self.token = add_parts(
                rows, picks, self.keep, self.got, list(needs)
            )
            self.got = [devices.far_swap(a, k + 1) for k, a in enumerate(self.sent)]
            self.deps = [self.keep, *self.sent]
        elif stage == last + 1:
            self.sent = self.total(token)
            self.got = [devices.far_swap(self.sent, k) for k in range(1, devices.ways)]
            self.deps = [self.sent]
        else:
            got = self.got if isinstance(self.got, list) else [self.got]
            if not isinstance(token, int):
                got = [jnp.where(token == 0, a, self.sent) for a in got]
            self.sent = jnp.concatenate([self.sent, *got], axis=0)
            self.got = devices.swap(self.sent, 2 * last + 1 - stage)
            self.deps = [self.sent]
        return self.deps

    def total(self, token):
        total = self.keep.astype(F32)
        for a in self.got:
            total = total + a.astype(F32)
        if not isinstance(token, int):
            total = jnp.where(token == 0, total, 0.0)
        return total.astype(BF16)

    def finish(self):
        while self.stage < 2 * self.devices.halvings + 1:
            self.advance()
        return self.sent, self.got


def on_device(
    tokens, segment_ids, w_qkv, b_qv, w_out, b_out, gain_one, shift_one,
    w_inner, b_inner, w_final, b_final, gain_two, shift_two, out_grad,
):
    parts, local_len, width = tokens.shape
    hidden = w_inner.shape[1]
    length = parts * local_len
    x = swap_rows(tokens, parts).reshape(length, width)
    segments = swap_rows(segment_ids, parts).reshape(length, 1)
    grads_in = swap_rows(out_grad, parts).reshape(length, width)

    slot = jnp.arange(PAIR, dtype=jnp.int32)[None, :]
    same = segments == slot
    kext = jnp.where(same | ((slot >= NSEG) & (slot < NSEG + 3)), 1.0, 0.0).astype(BF16)
    qext = jnp.where(same | (slot >= NSEG), 0.0, -FAR).astype(BF16)

    def row(vector):
        return vector.astype(F32).reshape(1, -1)

    devices = Slice(lax.axis_size("dp"), lax.axis_size("seq"))
    bit = jnp.asarray(devices.mine[0], jnp.int32).reshape(1)
    q, k, v, context, lse, xt = forward_attention(
        x, kext, qext, w_qkv, row(b_qv[0]), row(b_qv[1])
    )
    vectors = [
        row(v_) for v_ in (b_out, gain_one, shift_one, b_inner, b_final, gain_two, shift_two)
    ]
    (
        own_out, other_out, pooled, low, hat, inverse, grad_two, grad_final, slope, dw_final,
        gb_two,
    ) = forward_dense(
        context, x, grads_in, kext, w_out, w_inner, w_final, vectors
    )
    sum_final = lax.psum_scatter(dw_final, ("dp", "seq"), scatter_dimension=0, tiled=True)
    if parts == 2:
        me = lax.axis_index("seq")
        got = lax.ppermute(other_out, "seq", [(0, 1), (1, 0)])
        output_block = jnp.where(me == 0, jnp.stack([own_out, got]), jnp.stack([got, own_out]))
        other = lax.ppermute(pooled, "seq", [(0, 1), (1, 0)])
        pooled_all = jnp.where(me == 0, jnp.stack([pooled, other]), jnp.stack([other, pooled]))
    else:
        output = jnp.concatenate([own_out, other_out], axis=0)
        output_block = swap_back(output.reshape(parts, local_len, width), parts)
        pooled_all = lax.all_gather(pooled, "seq", axis=0)
    resid_grad, grad_context, grad_inner, attended, gb_one, gb_inner, token = backward_dense(
        grad_final, slope, grad_two, hat, inverse, w_out, w_inner, w_final, row(gain_one),
        [],
    )
    send, keep, token = dense_weights(
        bit, devices.padded(hidden + width + 32), low, grad_inner, context, attended,
        gb_one, gb_inner, gb_two, [output_block, pooled_all],
    )
    t_inner = Table(devices, send)
    t_inner.keep = keep
    heads = (q, k, v, grad_context, context)
    groups = width // GROUP
    qkv_rows = devices.padded(3 * width * groups + 8 * groups + 8)
    early, merged, biases = [], [], []
    for group in range(groups):
        last = group == groups - 1
        deps = t_inner.advance(token[0]) if group else t_inner.deps
        *found, token = backward_attention(
            group, bit, qkv_rows, biases if last else [], early if last else [],
            xt, kext, qext, lse, heads, deps,
        )
        merged.append(found[-1] if last else found[1])
        if not last:
            early.append(found[0])
            biases.append(found[2])
    t_qkv = Table(devices, found[0])
    t_qkv.keep = found[1]
    sum_final = jnp.where(token[0] == 0, sum_final, 0)
    all_final = lax.all_gather(sum_final, ("dp", "seq"), axis=0, tiled=True)
    own_x, other_x, token = input_grad(resid_grad, merged, w_qkv, [])
    while t_inner.stage < devices.halvings:
        t_inner.advance(token[0])
    if parts == 2:
        got = lax.ppermute(other_x, "seq", [(0, 1), (1, 0)]).astype(F32)
        input_block = jnp.where(me == 0, jnp.stack([own_x, got]), jnp.stack([got, own_x]))
    else:
        grad_x = jnp.concatenate([own_x.astype(BF16), other_x], axis=0)
        input_block = swap_back(grad_x.reshape(parts, local_len, width), parts).astype(F32)
    t_qkv.advance(token[0])
    while t_qkv.stage < devices.halvings:
        t_qkv.advance()
    sum_inner = t_inner.total(t_qkv.token[0])
    all_inner = lax.all_gather(sum_inner, ("dp", "seq"), axis=0, tiled=True)
    places = devices.places()
    wide_final, token = turn(all_final, [input_block])
    t_qkv.advance()
    t_qkv.advance(token[0])
    wide_qkv, small_qv = widen(
        widen_qkv_kernel, t_qkv.piece_rows, places, t_qkv.finish(),
        [(width, 3 * width), (8 * groups + 8, GROUP)], "widen_qkv",
    )
    order = devices.owners(lax.axis_size("dp"), lax.axis_size("seq"))
    wide_inner, wide_out, small = widen_inner(order, all_inner, hidden)

    gb_qv = jnp.stack(
        [jnp.concatenate([small_qv[8 * g + j] for g in range(groups)]) for j in range(2)]
    )
    return (
        output_block,
        pooled_all,
        input_block,
        wide_qkv,
        gb_qv,
        wide_out,
        small[2],
        small[0],
        small[1],
        wide_inner,
        small[8 : 8 + hidden // width].reshape(-1),
        wide_final,
        small[18],
        small[16],
        small[17],
    )


def solution(mesh):
    rows = P("dp", "seq", None)
    return jax.shard_map(
        on_device,
        mesh=mesh,
        in_specs=(rows, P("dp", "seq")) + (P(),) * 12 + (rows,),
        out_specs=(rows, P("dp", None, None), rows) + (P(),) * 12,
        check_vma=False,
    )
```

profile of v0, /device:TPU:13, one launch (start us, length us, event | category | flops | bytes accessed | tf_op | source)
XLA Modules:
  0.0 405.1 jit_solution(1559602201972107319)
XLA Ops:
  8.3 2.4 constant_dynamic-slice_fusion.5
  10.7 1.3 collective-permute-start
  17.7 11.5 %collective-permute-done = bf16[1,512,768]{2,1,0:T(8,128)(2,1)} collective-permute-done((bf16[1,512,768]{2,1,0:T(8,128)(2,1)}, bf16[1,512,768]{2,1,0:T(8,128)(2,1)}, u32[]{:S(2)}, u32[]{:S(2)}) %collective-permute-start) | collective-permute-done | bytes 786464 | tf_op jit(solution)/shard_map/ppermute | solution.py:803
  29.2 2.4 pad_maximum_fusion
  31.6 27.2 %attention_forward.1 = (bf16[1024,768]{1,0:T(8,128)(2,1)S(1)}, bf16[1024,768]{1,0:T(8,128)(2,1)S(1)}, bf16[1024,768]{1,0:T(8,128)(2,1)S(1)}, bf16[1024,768]{1,0:...) custom-call(bf16[1024,768]{1,0:T(8,128)(2,1)} %bitcast.65, ...), custom_call_target="tpu_custom_call" | custom-call | flops 24000000000 | bytes 16000000 | tf_op jit(solution)/shard_map/attention_forward/pallas_call | solution.py:154
  59.9 1.2 copy-done.13
  63.1 1.3 pad_maximum_fusion.1
  64.4 37.6 %dense_forward.1 = (bf16[512,768]{1,0:T(8,128)(2,1)}, bf16[512,768]{1,0:T(8,128)(2,1)}, f32[32,768]{1,0:T(8,128)}, bf16[768,1024]{1,0:T(8,128)(2,1)}, f32[1024,7...) custom-call(bf16[1024,768]{1,0:T(8,128)(2,1)} %get-tuple-element.71., ...), custom_call_target="tpu_custom_call" | custom-call | flops 44999999488 | bytes 45000000 | tf_op jit(solution)/shard_map/dense_forward/pallas_call | solution.py:497
  102.9 1.2 collective-permute-start.4
  104.4 23.1 %dense_backward.1 = (f32[1024,768]{1,0:T(8,128)}, bf16[1024,768]{1,0:T(8,128)(2,1)}, bf16[1024,3072]{1,0:T(8,128)(2,1)}, bf16[1024,768]{1,0:T(8,128)(2,1)}, f32[...) custom-call(bf16[1024,768]{1,0:T(8,128)(2,1)} %get-tuple-element.75.refs_0_, ...), custom_call_target="tpu_custom_call" | custom-call | flops 8000000000 | bytes 20000000 | tf_op jit(solution)/shard_map/dense_backward/pallas_call | solution.py:585
  127.6 1.4 maximum_select_fusion.1.refs_8_
  130.1 11.8 %dense_weights.1 = (bf16[2048,768]{1,0:T(8,128)(2,1)}, bf16[2048,768]{1,0:T(8,128)(2,1)}, s32[1]{0:T(128)}) custom-call(s32[1]{0:T(128)} %bitcast.7.refs_0_, bf16[768,1024]{1,0:T(8,128)(2,1)S(1)} %copy-done.11, bf16[1024,3072]{1,0:T(8,128)(2,1)} %get-tuple-element.88.refs_2_, bf16[1024,768]{1,0:T(8,128)(2,1)S(1)} %copy-done.10, ...), custom_call_target="tpu_custom_call" | custom-call | flops 6000000000 | bytes 16000000 | tf_op jit(solution)/shard_map/dense_weights/pallas_call | solution.py:659
  141.9 4.2 %collective-permute-start.5 = (bf16[2048,768]{1,0:T(8,128)(2,1)}, bf16[2048,768]{1,0:T(8,128)(2,1)}, u32[]{:S(2)}, u32[]{:S(2)}) collective-permute-start(bf16[2048,768]{1,0:T(8,128)(2,1)} %get-tuple-element.93.refs_10_), channel_id=1, source_target_pairs={{0,2},{1,3},{2,0},{3,1},{4,6},{5,7},{6,4},{7,5},{8,10},{9,11},{10,... | collective-permute-start | bytes 9437192 | tf_op jit(solution)/shard_map/ppermute | solution.py:845
  146.1 1.4 copy-done.15
  148.6 19.0 %attention_backward.3 = (bf16[2304,256]{1,0:T(8,128)(2,1)S(1)}, bf16[1024,768]{1,0:T(8,128)(2,1)S(1)}, f32[8,256]{1,0:T(8,128)S(1)}, s32[1]{0:T(128)}) custom-call(s32[1]{0:T(128)} %bitcast.7.refs_0_, bf16[768,1024]{1,0:T(8,128)(2,1)S(1)} %copy-done.15, bf16[1024,128]{1,0:T(8,128)(2,1)S(1)} %copy-done.2, ...), custom_call_target="tpu_custom_call" | custom-call | flops 8000000000 | bytes 10000000 | tf_op jit(solution)/shard_map/attention_backward/pallas_call | solution.py:321
  169.5 5.4 %add_convert_fusion = (bf16[1,1024,768]{2,1,0:T(8,128)(2,1)}, bf16[1024,768]{1,0:T(8,128)(2,1)}) fusion(bf16[2,1024,768]{2,1,0:T(8,128)(2,1)} %bitcast.10, s32[]{:T(128)S(6)} %select_n.135, bf16[2,1024,768]{2,1,0:T(8,128)(2,1)} %bitcast.63, s32[]{:T(128)S(6)} %select_n.134), kind=kLoop, calls=%fused_computation.1 | loop fusion | flops 6291456 | bytes 9437192 | tf_op jit(solution)/shard_map/convert_element_type | solution.py:921
  174.9 1.2 collective-permute-start.6
  177.2 19.2 %attention_backward.4 = (bf16[2304,256]{1,0:T(8,128)(2,1)S(1)}, bf16[1024,768]{1,0:T(8,128)(2,1)S(1)}, f32[8,256]{1,0:T(8,128)S(1)}, s32[1]{0:T(128)}) custom-call(s32[1]{0:T(128)} %bitcast.7.refs_0_, bf16[768,1024]{1,0:T(8,128)(2,1)S(1)} %copy-done.16, bf16[1024,128]{1,0:T(8,128)(2,1)S(1)} %copy-done.2, ...), custom_call_target="tpu_custom_call" | custom-call | flops 8000000000 | bytes 10000000 | tf_op jit(solution)/shard_map/attention_backward/pallas_call | solution.py:321
  199.2 3.2 fusion.3
  202.5 21.9 %attention_backward.5 = (bf16[3584,256]{1,0:T(8,128)(2,1)}, bf16[3584,256]{1,0:T(8,128)(2,1)}, bf16[1024,768]{1,0:T(8,128)(2,1)}, s32[1]{0:T(128)}) custom-call(s32[1]{0:T(128)} %bitcast.7.refs_0_, bf16[768,1024]{1,0:T(8,128)(2,1)} %get-tuple-element.81.refs_1_, bf16[1024,128]{1,0:T(8,128)(2,1)S(1)} %copy-done.2, ...), custom_call_target="tpu_custom_call" | custom-call | flops 8000000000 | bytes 10000000 | tf_op jit(solution)/shard_map/attention_backward/pallas_call | solution.py:321
  225.1 1.6 broadcast_select_fusion
  227.1 1.4 copy-done.6
  228.5 1.4 copy-done.8
  229.9 7.7 %input_grad.1 = (f32[512,768]{1,0:T(8,128)S(1)}, bf16[512,768]{1,0:T(8,128)(2,1)S(1)}, s32[1]{0:T(128)}) custom-call(f32[1024,768]{1,0:T(8,128)} %get-tuple-element.80.resid_ref, bf16[1024,768]{1,0:T(8,128)(2,1)S(1)} %copy-done.6, bf16[1024,768]{1,0:T(8,128)(2,1)S(1)} %copy-done.8, bf16[1024,768]{1,0:T(8,128)(2,1)} %get-tuple-element.103.m2_ref, ...), custom_call_target="tpu_custom_call" | custom-call | flops 4000000000 | bytes 16000000 | tf_op jit(solution)/shard_map/input_grad/pallas_call | solution.py:367
  239.2 3.7 add_convert_fusion.3
  242.9 1.2 collective-permute-start.9
  244.5 20.9 %collective-permute-done.9 = bf16[1792,256]{1,0:T(8,128)(2,1)S(1)} collective-permute-done((bf16[1792,256]{1,0:T(8,128)(2,1)}, bf16[1792,256]{1,0:T(8,128)(2,1)S(1)}, u32[]{:S(2)}, u32[]{:S(2)}) %collective-permute-start.9) | collective-permute-done | bytes 917536 | tf_op jit(solution)/shard_map/ppermute | solution.py:845
  266.3 2.4 fusion.7
  268.8 1.7 collective-permute-start.10
  271.2 2.0 add_parts.3
  273.3 2.4 collective-permute-start.22
  276.0 2.6 collective-permute-done.10.got_ref
  280.3 5.0 %collective-permute-done.21 = bf16[128,768]{1,0:T(8,128)(2,1)S(1)} collective-permute-done((bf16[128,768]{1,0:T(8,128)(2,1)}, bf16[128,768]{1,0:T(8,128)(2,1)S(1)}, u32[]{:S(2)}, u32[]{:S(2)}) %collective-permute-start.21) | collective-permute-done | bytes 196640 | tf_op jit(solution)/shard_map/ppermute | solution.py:848
  285.3 6.4 %collective-permute-done.22 = bf16[128,768]{1,0:T(8,128)(2,1)} collective-permute-done((bf16[128,768]{1,0:T(8,128)(2,1)}, bf16[128,768]{1,0:T(8,128)(2,1)}, u32[]{:S(2)}, u32[]{:S(2)}) %collective-permute-start.22) | collective-permute-done | bytes 196640 | tf_op jit(solution)/shard_map/ppermute | solution.py:848
  291.7 13.7 %collective-permute-done.23 = bf16[128,768]{1,0:T(8,128)(2,1)} collective-permute-done((bf16[128,768]{1,0:T(8,128)(2,1)}, bf16[128,768]{1,0:T(8,128)(2,1)}, u32[]{:S(2)}, u32[]{:S(2)}) %collective-permute-start.23) | collective-permute-done | bytes 196640 | tf_op jit(solution)/shard_map/ppermute | solution.py:848
  305.3 1.8 select_convert_fusion.2
  308.4 1.7 collective-permute-start.13
  310.2 16.3 %collective-permute-done.7 = bf16[512,768]{1,0:T(8,128)(2,1)S(1)} collective-permute-done((bf16[512,768]{1,0:T(8,128)(2,1)}, bf16[512,768]{1,0:T(8,128)(2,1)S(1)}, u32[]{:S(2)}, u32[]{:S(2)}) %collective-permute-start.7) | collective-permute-done | bytes 786464 | tf_op jit(solution)/shard_map/ppermute | solution.py:1039
  326.8 1.9 maximum_select_fusion.refs_0_
  328.7 3.5 collective-permute-start.15
  332.2 10.2 %turn.1 = (f32[3072,768]{1,0:T(8,128)}, s32[1]{0:T(128)}) custom-call(bf16[3072,768]{1,0:T(8,128)(2,1)} %all-gather.3.cloned.1.call-done.low_ref, f32[2,512,768]{2,1,0:T(8,128)} %maximum_select_fusion.refs_0_), custom_call_target="tpu_custom_call" | custom-call | bytes 14155776 | tf_op jit(solution)/shard_map/turn/pallas_call | solution.py:752
  343.5 7.4 %collective-permute-done.17 = bf16[896,256]{1,0:T(8,128)(2,1)S(1)} collective-permute-done((bf16[896,256]{1,0:T(8,128)(2,1)S(1)}, bf16[896,256]{1,0:T(8,128)(2,1)S(1)}, u32[]{:S(2)}, u32[]{:S(2)}) %collective-permute-start.17) | collective-permute-done | bytes 458784 | tf_op jit(solution)/shard_map/ppermute | solution.py:845
  351.4 24.2 %collective-permute-done.18 = bf16[1792,256]{1,0:T(8,128)(2,1)S(1)} collective-permute-done((bf16[1792,256]{1,0:T(8,128)(2,1)S(1)}, bf16[1792,256]{1,0:T(8,128)(2,1)S(1)}, u32[]{:S(2)}, u32[]{:S(2)}) %collective-permute-start.18) | collective-permute-done | bytes 917536 | tf_op jit(solution)/shard_map/ppermute | solution.py:845
  375.7 4.4 %collective-permute-start.19 = (bf16[3584,256]{1,0:T(8,128)(2,1)S(1)}, bf16[3584,256]{1,0:T(8,128)(2,1)}, u32[]{:S(2)}, u32[]{:S(2)}) collective-permute-start(bf16[3584,256]{1,0:T(8,128)(2,1)S(1)} %constant_dynamic-update-slice_fusion.5.refs_1_), channel_id=1, source_target_pairs={{0,2},{1,3},{2,0},{3,1},{4,6},{5,7},{6,4},{7,5},{8,10},{9,11},{10,... | collective-permute-start | bytes 5505032 | tf_op jit(solution)/shard_map/ppermute | solution.py:845
  380.1 3.5 collective-permute-done.19.refs_2_
  383.6 5.0 %widen_qkv.1 = (f32[768,2304]{1,0:T(8,128)}, f32[32,256]{1,0:T(8,128)S(1)}) custom-call(s32[4]{0:T(128)S(1)} %pad_add_fusion.refs_0_, bf16[3584,256]{1,0:T(8,128)(2,1)S(1)} %constant_dynamic-update-slice_fusion.5.refs_1_, bf16[3584,256]{1,0:T(8,128)(2,1)} %collective-permute-done.19.refs_2_), custom_call_target="tpu_custom_call" | custom-call | bytes 10780672 | tf_op jit(solution)/shard_map/widen_qkv/pallas_call | solution.py:786
  389.2 2.8 copy-done
  392.0 5.1 %widen_inner.1 = (f32[768,3072]{1,0:T(8,128)}, f32[768,768]{1,0:T(8,128)}, f32[32,768]{1,0:T(8,128)S(1)}) custom-call(bf16[4096,768]{1,0:T(8,128)(2,1)S(1)} %copy-done), custom_call_target="tpu_custom_call" | custom-call | bytes 18874368 | tf_op jit(solution)/shard_map/widen_inner/pallas_call | solution.py:733
  (149 shorter events, 26.2 us)
Async XLA Ops:
  7.2 4.8 %copy-start.26 = (bf16[2,512,768]{2,1,0:T(8,128)(2,1)S(1)}, bf16[2,512,768]{2,1,0:T(8,128)(2,1)}, u32[]{:S(2)}) copy-start(bf16[2,512,768]{2,1,0:T(8,128)(2,1)} %param.29) | copy-start | bytes 4718596
  7.2 217.9 %reduce-scatter.2.cloned.1.call-start = ((), (), s32[]{:S(2)}) async-start(), calls=%async_computation.1 | async-start | bytes 4866048 | tf_op jit(solution)/shard_map/reduce_scatter | solution.py:995
  8.1 9.3 %collective-permute-start.1 = (s32[1,512]{1,0:T(1,128)S(1)}, s32[1,512]{1,0:T(1,128)S(1)}, u32[]{:S(2)}, u32[]{:S(2)}) collective-permute-start(s32[1,512]{1,0:T(1,128)S(1)} %get-tuple-element.165), channel_id=1, source_target_pairs={{0,1},{1,0},{2,3},{3,2},{4,5},{5,4},{6,7},{7,6},{8,9},{9,8},{10,11... | collective-permute-start | bytes 6152 | tf_op jit(solution)/shard_map/ppermute | solution.py:803
  10.6 2.6 copy-start.30
  10.6 2.6 copy-start.32
  10.6 3.2 copy-start.33
  10.6 3.8 copy-start.34
  10.7 4.4 %copy-start.35 = (bf16[768]{0:T(1024)(128)(2,1)S(1)}, bf16[768]{0:T(1024)(128)(2,1)}, u32[]{:S(2)}) copy-start(bf16[768]{0:T(1024)(128)(2,1)} %param.26) | copy-start | bytes 4612
  10.7 4.9 %copy-start.36 = (bf16[768]{0:T(1024)(128)(2,1)S(1)}, bf16[768]{0:T(1024)(128)(2,1)}, u32[]{:S(2)}) copy-start(bf16[768]{0:T(1024)(128)(2,1)} %param.27) | copy-start | bytes 4612
  10.7 5.5 %copy-start.37 = (bf16[768]{0:T(1024)(128)(2,1)S(1)}, bf16[768]{0:T(1024)(128)(2,1)}, u32[]{:S(2)}) copy-start(bf16[768]{0:T(1024)(128)(2,1)} %param.28) | copy-start | bytes 4612
  10.7 6.1 %copy-start.31 = (bf16[3072]{0:T(1024)(128)(2,1)S(1)}, bf16[3072]{0:T(1024)(128)(2,1)}, u32[]{:S(2)}) copy-start(bf16[3072]{0:T(1024)(128)(2,1)} %param.24) | copy-start | bytes 18436
  10.7 18.5 %collective-permute-start = (bf16[1,512,768]{2,1,0:T(8,128)(2,1)}, bf16[1,512,768]{2,1,0:T(8,128)(2,1)}, u32[]{:S(2)}, u32[]{:S(2)}) collective-permute-start(bf16[1,512,768]{2,1,0:T(8,128)(2,1)} %get-tuple-element.152), channel_id=1, source_target_pairs={{0,1},{1,0},{2,3},{3,2},{4,5},{5,4},{6,7},{7,6},{8,9},{9,8},{10,11... | collective-permute-start | bytes 2359304 | tf_op jit(solution)/shard_map/ppermute | solution.py:803
  13.0 50.1 %collective-permute-start.2 = (bf16[1,512,768]{2,1,0:T(8,128)(2,1)}, bf16[1,512,768]{2,1,0:T(8,128)(2,1)S(1)}, u32[]{:S(2)}, u32[]{:S(2)}) collective-permute-start(bf16[1,512,768]{2,1,0:T(8,128)(2,1)} %get-tuple-element.150), channel_id=1, source_target_pairs={{0,1},{1,0},{2,3},{3,2},{4,5},{5,4},{6,7},{7,6},{8,9},{9,8},{10,11... | collective-permute-start | bytes 2359304 | tf_op jit(solution)/shard_map/ppermute | solution.py:803
  17.6 41.1 %copy-start.1 = (bf16[1024,128]{1,0:T(8,128)(2,1)}, bf16[1024,128]{1,0:T(8,128)(2,1)S(1)}, u32[]{:S(2)}) copy-start(bf16[1024,128]{1,0:T(8,128)(2,1)S(1)} %get-tuple-element.163.kext_ref.refs_2_) | copy-start | bytes 786436
  102.1 230.1 %all-gather.3.cloned.1.call-start = ((), (), s32[]{:S(2)}) async-start(), calls=%async_computation.2 | async-start | bytes 4866048 | tf_op jit(solution)/shard_map/all_gather | solution.py:1034
  102.9 24.7 %collective-permute-start.4 = (f32[32,768]{1,0:T(8,128)S(1)}, f32[32,768]{1,0:T(8,128)S(1)}, u32[]{:S(2)}, u32[]{:S(2)}) collective-permute-start(f32[32,768]{1,0:T(8,128)S(1)} %copy-done.29), channel_id=1, source_target_pairs={{0,1},{1,0},{2,3},{3,2},{4,5},{5,4},{6,7},{7,6},{8,9},{9,8},{10,11... | collective-permute-start | bytes 294920 | tf_op jit(solution)/shard_map/ppermute | solution.py:1000
  104.1 23.5 %collective-permute-start.3 = (bf16[512,768]{1,0:T(8,128)(2,1)S(1)}, bf16[512,768]{1,0:T(8,128)(2,1)S(1)}, u32[]{:S(2)}, u32[]{:S(2)}) collective-permute-start(bf16[512,768]{1,0:T(8,128)(2,1)S(1)} %copy-done.38), channel_id=1, source_target_pairs={{0,1},{1,0},{2,3},{3,2},{4,5},{5,4},{6,7},{7,6},{8,9},{9,8},{10,11... | collective-permute-start | bytes 2359304 | tf_op jit(solution)/shard_map/ppermute | solution.py:998
  104.4 23.2 %copy-start.28 = (bf16[512,768]{1,0:T(8,128)(2,1)S(1)}, bf16[512,768]{1,0:T(8,128)(2,1)}, u32[]{:S(2)}) copy-start(bf16[512,768]{1,0:T(8,128)(2,1)} %get-tuple-element.72) | copy-start | bytes 2359300
  104.4 24.6 %copy-start.11 = (bf16[768,1024]{1,0:T(8,128)(2,1)S(1)}, bf16[768,1024]{1,0:T(8,128)(2,1)}, u32[]{:S(2)}) copy-start(bf16[768,1024]{1,0:T(8,128)(2,1)} %get-tuple-element.87.refs_1_) | copy-start | bytes 4718596
  127.5 2.6 copy-start.10
  127.5 2.6 copy-start.23
  127.6 2.6 copy-start.24
  127.6 14.3 %copy-start.3 = (f32[2,32,768]{2,1,0:T(8,128)}, f32[2,32,768]{2,1,0:T(8,128)S(1)}, u32[]{:S(2)}) copy-start(f32[2,32,768]{2,1,0:T(8,128)S(1)} %maximum_select_fusion.2.refs_9_) | copy-start | bytes 589828
  130.1 16.0 %copy-start.2 = (bf16[1024,128]{1,0:T(8,128)(2,1)S(1)}, bf16[1024,128]{1,0:T(8,128)(2,1)}, u32[]{:S(2)}) copy-start(bf16[1024,128]{1,0:T(8,128)(2,1)} %copy-done.1) | copy-start | bytes 786436
  141.9 27.5 %collective-permute-start.5 = (bf16[2048,768]{1,0:T(8,128)(2,1)}, bf16[2048,768]{1,0:T(8,128)(2,1)}, u32[]{:S(2)}, u32[]{:S(2)}) collective-permute-start(bf16[2048,768]{1,0:T(8,128)(2,1)} %get-tuple-element.93.refs_10_), channel_id=1, source_target_pairs={{0,2},{1,3},{2,0},{3,1},{4,6},{5,7},{6,4},{7,5},{8,10},{9,11},{10,... | collective-permute-start | bytes 9437192 | tf_op jit(solution)/shard_map/ppermute | solution.py:845
  169.4 6.7 %copy-start.16 = (bf16[768,1024]{1,0:T(8,128)(2,1)S(1)}, bf16[768,1024]{1,0:T(8,128)(2,1)}, u32[]{:S(2)}) copy-start(bf16[768,1024]{1,0:T(8,128)(2,1)} %get-tuple-element.81.refs_1_) | copy-start | bytes 4718596
  174.9 24.3 %collective-permute-start.6 = (bf16[1024,768]{1,0:T(8,128)(2,1)}, bf16[1024,768]{1,0:T(8,128)(2,1)}, u32[]{:S(2)}, u32[]{:S(2)}) collective-permute-start(bf16[1024,768]{1,0:T(8,128)(2,1)} %get-tuple-element.142.refs_10_), channel_id=1, source_target_pairs={{0,4},{1,5},{2,3},{3,2},{4,0},{5,1},{6,7},{7,6},{8,12},{9,13},{10,... | collective-permute-start | bytes 4718600 | tf_op jit(solution)/shard_map/ppermute | solution.py:845
  199.2 3.3 copy-start.18
  199.2 3.2 copy-start.22
  226.7 162.5 %all-gather.5.cloned.1.call-start = ((), (), s32[]{:S(2)}) async-start(), calls=%async_computation.3 | async-start | bytes 6488064 | tf_op jit(solution)/shard_map/all_gather | solution.py:1048
  226.7 12.4 %collective-permute-start.8 = (bf16[3584,256]{1,0:T(8,128)(2,1)}, bf16[3584,256]{1,0:T(8,128)(2,1)}, u32[]{:S(2)}, u32[]{:S(2)}) collective-permute-start(bf16[3584,256]{1,0:T(8,128)(2,1)} %get-tuple-element.108), channel_id=1, source_target_pairs={{0,2},{1,3},{2,0},{3,1},{4,6},{5,7},{6,4},{7,5},{8,10},{9,11},{10,... | collective-permute-start | bytes 5505032 | tf_op jit(solution)/shard_map/ppermute | solution.py:845
  242.9 22.5 %collective-permute-start.9 = (bf16[1792,256]{1,0:T(8,128)(2,1)}, bf16[1792,256]{1,0:T(8,128)(2,1)S(1)}, u32[]{:S(2)}, u32[]{:S(2)}) collective-permute-start(bf16[1792,256]{1,0:T(8,128)(2,1)} %get-tuple-element.144), channel_id=1, source_target_pairs={{0,4},{1,5},{2,3},{3,2},{4,0},{5,1},{6,7},{7,6},{8,12},{9,13},{10,... | collective-permute-start | bytes 2752520 | tf_op jit(solution)/shard_map/ppermute | solution.py:845
  244.1 27.1 %collective-permute-start.20 = (bf16[512,768]{1,0:T(8,128)(2,1)}, bf16[512,768]{1,0:T(8,128)(2,1)}, u32[]{:S(2)}, u32[]{:S(2)}) collective-permute-start(bf16[512,768]{1,0:T(8,128)(2,1)} %get-tuple-element.146.refs_10_), channel_id=1, source_target_pairs={{0,1},{1,0},{2,6},{3,7},{4,5},{5,4},{6,2},{7,3},{8,9},{9,8},{10,14... | collective-permute-start | bytes 2359304 | tf_op jit(solution)/shard_map/ppermute | solution.py:845
  268.8 9.8 %collective-permute-start.10 = (bf16[896,256]{1,0:T(8,128)(2,1)}, bf16[896,256]{1,0:T(8,128)(2,1)S(1)}, u32[]{:S(2)}, u32[]{:S(2)}) collective-permute-start(bf16[896,256]{1,0:T(8,128)(2,1)} %get-tuple-element.147), channel_id=1, source_target_pairs={{0,1},{1,0},{2,6},{3,7},{4,5},{5,4},{6,2},{7,3},{8,9},{9,8},{10,14... | collective-permute-start | bytes 1376264 | tf_op jit(solution)/shard_map/ppermute | solution.py:845
  273.2 12.1 %collective-permute-start.21 = (bf16[128,768]{1,0:T(8,128)(2,1)}, bf16[128,768]{1,0:T(8,128)(2,1)S(1)}, u32[]{:S(2)}, u32[]{:S(2)}) collective-permute-start(bf16[128,768]{1,0:T(8,128)(2,1)} %get-tuple-element.120), channel_id=1, source_target_pairs={{0,8},{2,10},{4,12},{6,14},{8,0},{10,2},{12,4},{14,6},{16,24},{18,... | collective-permute-start | bytes 589832 | tf_op jit(solution)/shard_map/ppermute | solution.py:848
  273.3 18.3 %collective-permute-start.22 = (bf16[128,768]{1,0:T(8,128)(2,1)}, bf16[128,768]{1,0:T(8,128)(2,1)}, u32[]{:S(2)}, u32[]{:S(2)}) collective-permute-start(bf16[128,768]{1,0:T(8,128)(2,1)} %get-tuple-element.121), channel_id=1, source_target_pairs={{0,16},{2,18},{4,20},{6,22},{8,24},{10,26},{12,28},{14,30},{16,0},... | collective-permute-start | bytes 589832 | tf_op jit(solution)/shard_map/ppermute | solution.py:848
  275.7 29.6 %collective-permute-start.23 = (bf16[128,768]{1,0:T(8,128)(2,1)}, bf16[128,768]{1,0:T(8,128)(2,1)}, u32[]{:S(2)}, u32[]{:S(2)}) collective-permute-start(bf16[128,768]{1,0:T(8,128)(2,1)} %get-tuple-element.122), channel_id=1, source_target_pairs={{0,24},{2,26},{4,28},{6,30},{8,16},{10,18},{12,20},{14,22},{16,8},... | collective-permute-start | bytes 589832 | tf_op jit(solution)/shard_map/ppermute | solution.py:848
  307.2 19.3 %collective-permute-start.7 = (bf16[512,768]{1,0:T(8,128)(2,1)}, bf16[512,768]{1,0:T(8,128)(2,1)S(1)}, u32[]{:S(2)}, u32[]{:S(2)}) collective-permute-start(bf16[512,768]{1,0:T(8,128)(2,1)} %copy-done.4), channel_id=1, source_target_pairs={{0,1},{1,0},{2,3},{3,2},{4,5},{5,4},{6,7},{7,6},{8,9},{9,8},{10,11... | collective-permute-start | bytes 2359304 | tf_op jit(solution)/shard_map/ppermute | solution.py:1039
  307.5 19.1 %collective-permute-start.11 = (bf16[224,256]{1,0:T(8,128)(2,1)S(1)}, bf16[224,256]{1,0:T(8,128)(2,1)S(1)}, u32[]{:S(2)}, u32[]{:S(2)}) collective-permute-start(bf16[224,256]{1,0:T(8,128)(2,1)S(1)} %get-tuple-element.110), channel_id=1, source_target_pairs={{0,8},{2,10},{4,12},{6,14},{8,0},{10,2},{12,4},{14,6},{16,24},{18,... | collective-permute-start | bytes 344072 | tf_op jit(solution)/shard_map/ppermute | solution.py:848
  307.5 19.1 %collective-permute-start.12 = (bf16[224,256]{1,0:T(8,128)(2,1)S(1)}, bf16[224,256]{1,0:T(8,128)(2,1)S(1)}, u32[]{:S(2)}, u32[]{:S(2)}) collective-permute-start(bf16[224,256]{1,0:T(8,128)(2,1)S(1)} %get-tuple-element.111), channel_id=1, source_target_pairs={{0,16},{2,18},{4,20},{6,22},{8,24},{10,26},{12,28},{14,30},{16,0},... | collective-permute-start | bytes 344072 | tf_op jit(solution)/shard_map/ppermute | solution.py:848
  308.4 18.2 %collective-permute-start.13 = (bf16[224,256]{1,0:T(8,128)(2,1)S(1)}, bf16[224,256]{1,0:T(8,128)(2,1)S(1)}, u32[]{:S(2)}, u32[]{:S(2)}) collective-permute-start(bf16[224,256]{1,0:T(8,128)(2,1)S(1)} %get-tuple-element.112), channel_id=1, source_target_pairs={{0,24},{2,26},{4,28},{6,30},{8,16},{10,18},{12,20},{14,22},{16,8},... | collective-permute-start | bytes 344072 | tf_op jit(solution)/shard_map/ppermute | solution.py:848
  326.7 16.3 %collective-permute-start.14 = (bf16[224,256]{1,0:T(8,128)(2,1)S(1)}, bf16[224,256]{1,0:T(8,128)(2,1)S(1)}, u32[]{:S(2)}, u32[]{:S(2)}) collective-permute-start(bf16[224,256]{1,0:T(8,128)(2,1)S(1)} %get-tuple-element.140), channel_id=1, source_target_pairs={{0,8},{2,10},{4,12},{6,14},{8,0},{10,2},{12,4},{14,6},{16,24},{18,... | collective-permute-start | bytes 344072 | tf_op jit(solution)/shard_map/ppermute | solution.py:848
  328.7 14.4 %collective-permute-start.16 = (bf16[224,256]{1,0:T(8,128)(2,1)S(1)}, bf16[224,256]{1,0:T(8,128)(2,1)S(1)}, u32[]{:S(2)}, u32[]{:S(2)}) collective-permute-start(bf16[224,256]{1,0:T(8,128)(2,1)S(1)} %get-tuple-element.140), channel_id=1, source_target_pairs={{0,24},{2,26},{4,28},{6,30},{8,16},{10,18},{12,20},{14,22},{16,8},... | collective-permute-start | bytes 344072 | tf_op jit(solution)/shard_map/ppermute | solution.py:848
  328.7 14.4 %collective-permute-start.15 = (bf16[224,256]{1,0:T(8,128)(2,1)S(1)}, bf16[224,256]{1,0:T(8,128)(2,1)S(1)}, u32[]{:S(2)}, u32[]{:S(2)}) collective-permute-start(bf16[224,256]{1,0:T(8,128)(2,1)S(1)} %get-tuple-element.140), channel_id=1, source_target_pairs={{0,16},{2,18},{4,20},{6,22},{8,24},{10,26},{12,28},{14,30},{16,0},... | collective-permute-start | bytes 344072 | tf_op jit(solution)/shard_map/ppermute | solution.py:848
  343.2 7.7 %collective-permute-start.17 = (bf16[896,256]{1,0:T(8,128)(2,1)S(1)}, bf16[896,256]{1,0:T(8,128)(2,1)S(1)}, u32[]{:S(2)}, u32[]{:S(2)}) collective-permute-start(bf16[896,256]{1,0:T(8,128)(2,1)S(1)} %pad_maximum_fusion.2), channel_id=1, source_target_pairs={{0,1},{1,0},{2,6},{3,7},{4,5},{5,4},{6,2},{7,3},{8,9},{9,8},{10,14... | collective-permute-start | bytes 1376264 | tf_op jit(solution)/shard_map/ppermute | solution.py:845
  351.0 24.6 %collective-permute-start.18 = (bf16[1792,256]{1,0:T(8,128)(2,1)S(1)}, bf16[1792,256]{1,0:T(8,128)(2,1)S(1)}, u32[]{:S(2)}, u32[]{:S(2)}) collective-permute-start(bf16[1792,256]{1,0:T(8,128)(2,1)S(1)} %get-tuple-element.153), channel_id=1, source_target_pairs={{0,4},{1,5},{2,3},{3,2},{4,0},{5,1},{6,7},{7,6},{8,12},{9,13},{10,... | collective-permute-start | bytes 2752520 | tf_op jit(solution)/shard_map/ppermute | solution.py:845
  375.7 7.9 %collective-permute-start.19 = (bf16[3584,256]{1,0:T(8,128)(2,1)S(1)}, bf16[3584,256]{1,0:T(8,128)(2,1)}, u32[]{:S(2)}, u32[]{:S(2)}) collective-permute-start(bf16[3584,256]{1,0:T(8,128)(2,1)S(1)} %constant_dynamic-update-slice_fusion.5.refs_1_), channel_id=1, source_target_pairs={{0,2},{1,3},{2,0},{3,1},{4,6},{5,7},{6,4},{7,5},{8,10},{9,11},{10,... | collective-permute-start | bytes 5505032 | tf_op jit(solution)/shard_map/ppermute | solution.py:845
  389.2 2.8 copy-start
  (18 other events, 23.4 us)
Sparse Core Ops, SparseCore 0:
  102.2 111.2 reduce-scatter.1
  226.8 75.8 all-gather.2
  307.3 79.5 all-gather.4
where the time goes:
time: 413 us; the launch traced here: 405 us
  Pallas kernels  191 us (46%)
  waiting for transfers between devices  112 us (27%)
  local copies, waits for them, and re-layouts  29.6 us (7%)
  other arithmetic  27.2 us (7%)
  starting transfers between devices  26.9 us (7%)
  between operations  19.1 us (5%)
    pallas_call x3, Pallas kernels, backward_attention(): pl.pallas_call(kernel, grid=(1,), in_specs=[pl.BlockSpec(memory_space=plt...  60.1 us
    ppermute x9, waiting for transfers between devices, swap(): return lax.ppermute(array, ('dp', 'seq'), self.pairs[stage])  58.6 us
    pallas_call x1, Pallas kernels, forward_dense(): pl.pallas_call(forward_dense_kernel, grid=(length // TOKENS,), in_specs=[...  37.6 us
    pallas_call x1, Pallas kernels, forward_attention(): pl.pallas_call(forward_attention_kernel, grid=(groups,), in_specs=[whole(...  27.2 us
    ppermute x9, waiting for transfers between devices, far_swap(): return lax.ppermute(array, 'dp', self.far_pairs[k])  25 us
    pallas_call x1, Pallas kernels, backward_dense(): pl.pallas_call(kernel, grid=(length // TOKENS,), in_specs=[rows_of(TOKENS...  23.1 us
    unnamed x82, local copies, waits for them, and re-layouts  20.6 us
    ppermute x1, waiting for transfers between devices, on_device(): got = lax.ppermute(other_x, 'seq', [(0, 1), (1, 0)]).astype(F32)  16.3 us
  transfers between devices with their start and end apart: 27, of which 10 were waited for; matrix products, arithmetic and copies ran while one was open for 8% of the time, Pallas kernels for 37%

commit v1 on v0

--- a/solution.py
+++ b/solution.py
@@ -176,7 +176,7 @@
             pltpu.VMEM((2, length, 2 * PAIR), BF16),
             pltpu.VMEM((4, length, PAIR), BF16),
         ],
-        compiler_params=params(48),
+        compiler_params=params(60),
         cost_estimate=cost(24 * 10**9, 16 * 10**6, HEADS * length * length),
         name="attention_forward",
     )(x, kext, qext, w_qkv, w_qkv, w_qkv, bias_q, bias_v)
@@ -333,7 +333,7 @@
             pltpu.VMEM((length, PAIR), F32),
         ],
         out_shape=[shape(*o) for o in outs] + [shape((1,), jnp.int32)],
-        compiler_params=params(48),
+        compiler_params=params(60),
         cost_estimate=cost(8 * 10**9, 10 * 10**6, 4 * length * length),
         name="attention_backward",
     )(bit, *operands)
@@ -381,7 +381,7 @@
             shape((length // 2, width), BF16),
             shape((1,), jnp.int32),
         ],
-        compiler_params=params(48),
+        compiler_params=params(60),
         cost_estimate=cost(4 * 10**9, 16 * 10**6),
         name="input_grad",
     )(resid, *merged, w_qkv, *deps)
@@ -533,7 +533,7 @@
             pltpu.VMEM((PAIR, PAIR), F32),
             pltpu.VMEM((2, TOKENS, CHUNK), F32),
         ],
-        compiler_params=params(56),
+        compiler_params=params(60),
         cost_estimate=cost(45 * 10**9, 45 * 10**6, length * hidden),
         name="dense_forward",
     )(context, x, out_grad, kext, w_out, w_inner, w_final, *vectors)
@@ -615,7 +615,7 @@
             shape((8, width), F32),
             shape((1,), jnp.int32),
         ],
-        compiler_params=params(56),
+        compiler_params=params(60),
         cost_estimate=cost(8 * 10**9, 20 * 10**6),
         name="dense_backward",
     )(final, slope, grad_two, hat, inverse, w_out, w_inner, w_final, gain, *deps)
@@ -674,7 +674,7 @@
         out_shape=[jax.ShapeDtypeStruct((rows // 2, width), BF16)] * 2
         + [jax.ShapeDtypeStruct((1,), jnp.int32)],
         scratch_shapes=[pltpu.VMEM((rows, width), BF16)],
-        compiler_params=params(48),
+        compiler_params=params(60),
         cost_estimate=cost(6 * 10**9, 16 * 10**6),
         name="dense_weights",
     )(bit, low, inner, context, attended, gb_one, gb_inner, gb_two, *deps)
@@ -707,64 +707,78 @@
         small_ref[row : row + count, :] = values[:count, :]
 
 
-def widen_inner_kernel(order, table_ref, inner_ref, out_ref, small_ref):
+def widen_dense_kernel(rows, piece_of, table_ref, final_ref, inner_ref, out_ref, small_ref, square):
     width, hidden = inner_ref.shape
-    rows = table_ref.shape[0] // len(order)
-    for piece, device in enumerate(order):
-        at = 0
-        while at < rows:
-            start = piece * rows + at
-            count = min(rows - at, width - start % width)
-            here = table_ref[device * rows + at : device * rows + at + count, :].astype(F32)
-            block, row = start // width, start % width
-            if start < hidden:
-                inner_ref[row : row + count, block * width : (block + 1) * width] = here
-            elif start < hidden + width:
-                out_ref[row : row + count, :] = here
-            else:
-                put_small(small_ref, start - hidden - width, here)
-            at += count
-
-
-def widen_inner(order, table, hidden):
+    first, second = rows
+    count = width // first
+    for i in range(count):
+        at = i * (first + second)
+        square[i * first : (i + 1) * first, :] = table_ref[at : at + first, :]
+        here = slice(at + first, at + first + second)
+        start = piece_of[pl.program_id(0) * count + i] * second
+        row = pl.ds(pl.multiple_of(start % width, second), second)
+
+        @pl.when(start < hidden)
+        def _():
+            block = pl.ds(pl.multiple_of(start // width * width, width), width)
+            inner_ref[row, block] = table_ref[here, :].astype(F32)
+
+        @pl.when((start >= hidden) & (start < hidden + width))
+        def _():
+            out_ref[row, :] = table_ref[here, :].astype(F32)
+
+        @pl.when(start == hidden + width)
+        def _():
+            small_ref[...] = table_ref[at + first : at + first + small_ref.shape[0], :].astype(F32)
+
+    for r in range(0, width, UNIT):
+        final_ref[r : r + UNIT, :] = square[:, r : r + UNIT].astype(F32).T
+
+
+def widen_dense(owners, rows, table, hidden):
     width = table.shape[1]
-    vmem = pl.BlockSpec(memory_space=pltpu.VMEM)
-    shapes = [(width, hidden), (width, width), (32, width)]
-    return pl.pallas_call(
-        lambda *refs: widen_inner_kernel(order, *refs),
-        in_specs=[vmem],
-        out_specs=[vmem] * 3,
-        out_shape=[jax.ShapeDtypeStruct(s, F32) for s in shapes],
-        compiler_params=pltpu.CompilerParams(vmem_limit_bytes=40 * 2**20),
-        cost_estimate=cost(0, 6 * table.size),
-        name="widen_inner",
-    )(table)
-
-
-def turn_kernel(low_ref, *refs):
-    refs[-1][0] = 0
-    refs[-2][...] = low_ref[...].astype(F32).T
-
-
-def turn(table, deps):
-    rows, width = table.shape
-    per = width // UNIT
-    return pl.pallas_call(
-        turn_kernel,
-        grid=(rows // width, per),
-        in_specs=[pl.BlockSpec((width, UNIT), lambda b, r: (b, r))]
-        + [pl.BlockSpec(memory_space=pl.ANY)] * len(deps),
-        out_specs=[
-            pl.BlockSpec((UNIT, width), lambda b, r: (b * per + r, 0)),
-            pl.BlockSpec(memory_space=pltpu.SMEM),
-        ],
-        out_shape=[
-            jax.ShapeDtypeStruct((rows, width), F32),
-            jax.ShapeDtypeStruct((1,), jnp.int32),
-        ],
-        cost_estimate=cost(0, 6 * rows * width),
-        name="turn",
-    )(table, *deps)
+    first, second = rows
+    count = len(owners)
+    if first * count == hidden and first % 16 == 0 and width % first == 0 and width % second == 0:
+        piece_of = [0] * count
+        for piece, device in enumerate(owners):
+            piece_of[device] = piece
+        shape = jax.ShapeDtypeStruct
+        return pl.pallas_call(
+            lambda *refs: widen_dense_kernel(rows, *refs),
+            grid=(hidden // width,),
+            in_specs=[
+                pl.BlockSpec(memory_space=pltpu.SMEM),
+                rows_of(width // first * (first + second), width),
+            ],
+            out_specs=[
+                rows_of(width, width),
+                whole((width, hidden)),
+                whole((width, width)),
+                whole((32, width)),
+            ],
+            out_shape=[
+                shape((hidden, width), F32),
+                shape((width, hidden), F32),
+                shape((width, width), F32),
+                shape((32, width), F32),
+            ],
+            scratch_shapes=[pltpu.VMEM((width, width), BF16)],
+            compiler_params=params(48),
+            cost_estimate=cost(0, 6 * table.size),
+            name="widen_dense",
+        )(jnp.array(piece_of, jnp.int32), table)
+    pieces = table.reshape(count, first + second, width)
+    squares = pieces[:, :first].reshape(hidden // width, width, width).astype(F32)
+    other = jnp.concatenate([pieces[device, first:] for device in owners]).astype(F32)
+    inner = other[:hidden].reshape(hidden // width, width, width)
+    at = hidden + width
+    return (
+        squares.transpose(0, 2, 1).reshape(hidden, width),
+        inner.transpose(1, 0, 2).reshape(width, hidden),
+        other[hidden:at],
+        other[at : at + 32],
+    )
 
 
 def widen_qkv_kernel(rows, scalars, own_ref, other_ref, out_ref, small_ref):
@@ -795,11 +809,11 @@
     )(scalars, *arrays)
 
 
-def swap_rows(array, parts):
+def swap_rows(array, parts, after=0):
     if parts == 2:
         me = lax.axis_index("seq")
         own = lax.dynamic_index_in_dim(array, me, 0, keepdims=True)
-        other = lax.dynamic_index_in_dim(array, 1 - me, 0, keepdims=True)
+        other = lax.dynamic_index_in_dim(array, 1 - me + after, 0, keepdims=True)
         got = lax.ppermute(other, "seq", [(0, 1), (1, 0)])
         return jnp.concatenate([own, got], axis=0)
     return lax.all_to_all(array, "seq", split_axis=0, concat_axis=0, tiled=True)
@@ -968,7 +982,8 @@
     length = parts * local_len
     x = swap_rows(tokens, parts).reshape(length, width)
     segments = swap_rows(segment_ids, parts).reshape(length, 1)
-    grads_in = swap_rows(out_grad, parts).reshape(length, width)
+    came = x[length - 1, width - 1]
+    grads_in = swap_rows(out_grad, parts, (came != came).astype(jnp.int32)).reshape(length, width)
 
     slot = jnp.arange(PAIR, dtype=jnp.int32)[None, :]
     same = segments == slot
@@ -1030,11 +1045,7 @@
             biases.append(found[2])
     t_qkv = Table(devices, found[0])
     t_qkv.keep = found[1]
-    sum_final = jnp.where(token[0] == 0, sum_final, 0)
-    all_final = lax.all_gather(sum_final, ("dp", "seq"), axis=0, tiled=True)
     own_x, other_x, token = input_grad(resid_grad, merged, w_qkv, [])
-    while t_inner.stage < devices.halvings:
-        t_inner.advance(token[0])
     if parts == 2:
         got = lax.ppermute(other_x, "seq", [(0, 1), (1, 0)]).astype(F32)
         input_block = jnp.where(me == 0, jnp.stack([own_x, got]), jnp.stack([got, own_x]))
@@ -1042,20 +1053,21 @@
         grad_x = jnp.concatenate([own_x.astype(BF16), other_x], axis=0)
         input_block = swap_back(grad_x.reshape(parts, local_len, width), parts).astype(F32)
     t_qkv.advance(token[0])
+    while t_inner.stage < devices.halvings:
+        t_inner.advance(token[0], t_qkv.deps)
     while t_qkv.stage < devices.halvings:
-        t_qkv.advance()
-    sum_inner = t_inner.total(t_qkv.token[0])
-    all_inner = lax.all_gather(sum_inner, ("dp", "seq"), axis=0, tiled=True)
+        t_qkv.advance(t_inner.token[0], [input_block])
+    pieces = (sum_final.shape[0], t_inner.piece_rows)
+    all_dense = lax.all_gather(
+        jnp.concatenate([sum_final, t_inner.total(0)]), ("dp", "seq"), axis=0, tiled=True
+    )
     places = devices.places()
-    wide_final, token = turn(all_final, [input_block])
-    t_qkv.advance()
-    t_qkv.advance(token[0])
     wide_qkv, small_qv = widen(
         widen_qkv_kernel, t_qkv.piece_rows, places, t_qkv.finish(),
         [(width, 3 * width), (8 * groups + 8, GROUP)], "widen_qkv",
     )
-    order = devices.owners(lax.axis_size("dp"), lax.axis_size("seq"))
-    wide_inner, wide_out, small = widen_inner(order, all_inner, hidden)
+    owners = devices.owners(lax.axis_size("dp"), lax.axis_size("seq"))
+    wide_final, wide_inner, wide_out, small = widen_dense(owners, pieces, all_dense, hidden)
 
     gb_qv = jnp.stack(
         [jnp.concatenate([small_qv[8 * g + j] for g in range(groups)]) for j in range(2)]

time: 413 us -> 404 us (0.978)
  local copies, waits for them, and re-layouts: 29.6 us -> 11.8 us
  waiting for transfers between devices: 112 us -> 127 us
  other arithmetic: 27.2 us -> 18.4 us
  Pallas kernels: 191 us -> 197 us
    ppermute x9, waiting for transfers between devices: 25 us -> 53.5 us  [far_swap(): return lax.ppermute(array, 'dp', self.far_pairs[k])]
    unnamed x82 -> x49, local copies, waits for them, and re-layouts: 20.6 us -> 3.88 us
    ppermute x9, waiting for transfers between devices: 58.6 us -> 43.2 us  [swap(): return lax.ppermute(array, ('dp', 'seq'), self.pairs[stage])]
    pallas_call x3, Pallas kernels: 60.1 us -> 65.5 us  [backward_attention(): pl.pallas_call(kernel, grid=(1,), in_specs=[pl.BlockSpec(memory_space=plt...]
    convert_element_type x4, other arithmetic: 14.8 us -> 9.65 us  [added(): return (parts[0] + parts[1]).astype(BF16)]
    pallas_call x2 -> x1, Pallas kernels: 15.3 us -> 12.9 us  [widen_dense(): pl.pallas_call(lambda *refs: widen_dense_kernel(rows, *refs), grid=(hidde...]
  transfers between devices with their start and end apart: 27 -> 26, of which waited for: 10 -> 16; matrix products, arithmetic and copies ran while one was open for 8% -> 4% of each run, Pallas kernels for 37% -> 33%
where the time goes in v1:
time: 404 us; the launch traced here: 399 us
  Pallas kernels  197 us (49%)
  waiting for transfers between devices  127 us (31%)
  starting transfers between devices  25.1 us (6%)
  between operations  19.9 us (5%)
  other arithmetic  18.4 us (5%)
  local copies, waits for them, and re-layouts  11.8 us (3%)
    pallas_call x3, Pallas kernels, backward_attention(): pl.pallas_call(kernel, grid=(1,), in_specs=[pl.BlockSpec(memory_space=plt...  65.5 us
    ppermute x9, waiting for transfers between devices, far_swap(): return lax.ppermute(array, 'dp', self.far_pairs[k])  53.5 us
    ppermute x9, waiting for transfers between devices, swap(): return lax.ppermute(array, ('dp', 'seq'), self.pairs[stage])  43.2 us
    pallas_call x1, Pallas kernels, forward_dense(): pl.pallas_call(forward_dense_kernel, grid=(length // TOKENS,), in_specs=[...  37.6 us
    pallas_call x1, Pallas kernels, forward_attention(): pl.pallas_call(forward_attention_kernel, grid=(groups,), in_specs=[whole(...  28 us
    pallas_call x1, Pallas kernels, backward_dense(): pl.pallas_call(kernel, grid=(length // TOKENS,), in_specs=[rows_of(TOKENS...  23 us
    ppermute x1, waiting for transfers between devices, on_device(): got = lax.ppermute(other_x, 'seq', [(0, 1), (1, 0)]).astype(F32)  16.9 us
    pallas_call x1, Pallas kernels, dense_weights(): pl.pallas_call(kernel, grid=(blocks + 1,), in_specs=[pl.BlockSpec(memory_...  13.2 us
  transfers between devices with their start and end apart: 26, of which 16 were waited for; matrix products, arithmetic and copies ran while one was open for 4% of the time, Pallas kernels for 33%

profile of v1, /device:TPU:13, one launch (start us, length us, event | category | flops | bytes accessed | tf_op | source)
XLA Modules:
  0.0 399.0 jit_solution(3323705473150464359)
XLA Ops:
  7.3 2.4 constant_dynamic-slice_fusion.5
  9.9 1.3 collective-permute-start.1
  15.9 12.4 %collective-permute-done.1 = s32[1,512]{1,0:T(1,128)S(1)} collective-permute-done((s32[1,512]{1,0:T(1,128)S(1)}, s32[1,512]{1,0:T(1,128)S(1)}, u32[]{:S(2)}, u32[]{:S(2)}) %collective-permute-start.1) | collective-permute-done | bytes 2080 | tf_op jit(solution)/shard_map/ppermute | solution.py:817
  29.6 1.1 copy-done.8
  33.0 28.0 %attention_forward.1 = (bf16[1024,768]{1,0:T(8,128)(2,1)}, bf16[1024,768]{1,0:T(8,128)(2,1)}, bf16[1024,768]{1,0:T(8,128)(2,1)}, bf16[1024,768]{1,0:T(8,128)(2,1...) custom-call(bf16[1024,768]{1,0:T(8,128)(2,1)} %bitcast.68, bf16[1024,128]{1,0:T(8,128)(2,1)} %get-tuple-element.158.kext_ref.refs_2_, ...), custom_call_target="tpu_custom_call" | custom-call | flops 24000000000 | bytes 16000000 | tf_op jit(solution)/shard_map/attention_forward/pallas_call | solution.py:154
  61.0 1.3 pad_maximum_fusion.1
  62.3 37.6 %dense_forward.1 = (bf16[512,768]{1,0:T(8,128)(2,1)}, bf16[512,768]{1,0:T(8,128)(2,1)}, f32[32,768]{1,0:T(8,128)}, bf16[768,1024]{1,0:T(8,128)(2,1)}, f32[1024,7...) custom-call(bf16[1024,768]{1,0:T(8,128)(2,1)} %get-tuple-element.69., ...), custom_call_target="tpu_custom_call" | custom-call | flops 44999999488 | bytes 45000000 | tf_op jit(solution)/shard_map/dense_forward/pallas_call | solution.py:497
  100.0 1.3 collective-permute-start.4
  101.5 23.0 %dense_backward.1 = (f32[1024,768]{1,0:T(8,128)}, bf16[1024,768]{1,0:T(8,128)(2,1)}, bf16[1024,3072]{1,0:T(8,128)(2,1)}, bf16[1024,768]{1,0:T(8,128)(2,1)}, f32[...) custom-call(bf16[1024,768]{1,0:T(8,128)(2,1)} %get-tuple-element.73.refs_0_, ...), custom_call_target="tpu_custom_call" | custom-call | flops 8000000000 | bytes 20000000 | tf_op jit(solution)/shard_map/dense_backward/pallas_call | solution.py:585
  125.2 1.4 maximum_select_fusion.1.refs_8_
  126.6 13.2 %dense_weights.1 = (bf16[2048,768]{1,0:T(8,128)(2,1)}, bf16[2048,768]{1,0:T(8,128)(2,1)}, s32[1]{0:T(128)}) custom-call(s32[1]{0:T(128)} %bitcast.8.refs_0_, bf16[768,1024]{1,0:T(8,128)(2,1)} %get-tuple-element.85.refs_1_, bf16[1024,3072]{1,0:T(8,128)(2,1)} %get-tuple-element.86.refs_2_, bf16[1024,768]{1,0:T(8,128)(2,1)} %get-tuple-element.69.ctx_ref.refs_3_.refs_9_, ...), custom_call_target="tpu_custom_call" | custom-call | flops 6000000000 | bytes 16000000 | tf_op jit(solution)/shard_map/dense_weights/pallas_call | solution.py:659
  139.8 2.5 collective-permute-start.5
  142.3 21.0 %attention_backward.3 = (bf16[2304,256]{1,0:T(8,128)(2,1)}, bf16[1024,768]{1,0:T(8,128)(2,1)}, f32[8,256]{1,0:T(8,128)}, s32[1]{0:T(128)}) custom-call(s32[1]{0:T(128)} %bitcast.8.refs_0_, bf16[768,1024]{1,0:T(8,128)(2,1)} %get-tuple-element.79.refs_1_, bf16[1024,128]{1,0:T(8,128)(2,1)} %get-tuple-element.158.kext_ref.refs_2_, ...), custom_call_target="tpu_custom_call" | custom-call | flops 8000000000 | bytes 10000000 | tf_op jit(solution)/shard_map/attention_backward/pallas_call | solution.py:321
  164.1 4.4 %add_convert_fusion = (bf16[1,1024,768]{2,1,0:T(8,128)(2,1)}, bf16[1024,768]{1,0:T(8,128)(2,1)}) fusion(bf16[2,1024,768]{2,1,0:T(8,128)(2,1)} %bitcast.11, s32[]{:T(128)S(6)} %select_n.106, bf16[2,1024,768]{2,1,0:T(8,128)(2,1)S(1)} %bitcast.63, s32[]{:T(128)S(6)} %select_n.105), kind=kLoop, calls=%fused_computation.1 | loop fusion | flops 6291456 | bytes 9437192 | tf_op jit(solution)/shard_map/convert_element_type | solution.py:935
  168.4 1.2 collective-permute-start.6
  169.7 21.4 %attention_backward.4 = (bf16[2304,256]{1,0:T(8,128)(2,1)}, bf16[1024,768]{1,0:T(8,128)(2,1)}, f32[8,256]{1,0:T(8,128)}, s32[1]{0:T(128)}) custom-call(s32[1]{0:T(128)} %bitcast.8.refs_0_, bf16[768,1024]{1,0:T(8,128)(2,1)} %get-tuple-element.79.refs_1_, bf16[1024,128]{1,0:T(8,128)(2,1)} %get-tuple-element.158.kext_ref.refs_2_, ...), custom_call_target="tpu_custom_call" | custom-call | flops 8000000000 | bytes 10000000 | tf_op jit(solution)/shard_map/attention_backward/pallas_call | solution.py:321
  191.8 1.6 fusion.3
  193.3 23.0 %attention_backward.5 = (bf16[3584,256]{1,0:T(8,128)(2,1)}, bf16[3584,256]{1,0:T(8,128)(2,1)}, bf16[1024,768]{1,0:T(8,128)(2,1)}, s32[1]{0:T(128)}) custom-call(s32[1]{0:T(128)} %bitcast.8.refs_0_, bf16[768,1024]{1,0:T(8,128)(2,1)} %get-tuple-element.79.refs_1_, bf16[1024,128]{1,0:T(8,128)(2,1)} %get-tuple-element.158.kext_ref.refs_2_, ...), custom_call_target="tpu_custom_call" | custom-call | flops 8000000000 | bytes 10000000 | tf_op jit(solution)/shard_map/attention_backward/pallas_call | solution.py:321
  217.7 9.4 %input_grad.1 = (f32[512,768]{1,0:T(8,128)}, bf16[512,768]{1,0:T(8,128)(2,1)}, s32[1]{0:T(128)}) custom-call(f32[1024,768]{1,0:T(8,128)} %get-tuple-element.78.resid_ref, bf16[1024,768]{1,0:T(8,128)(2,1)} %get-tuple-element.92.m0_ref, bf16[1024,768]{1,0:T(8,128)(2,1)} %get-tuple-element.95.m1_ref, bf16[1024,768]{1,0:T(8,128)(2,1)} %get-tuple-element.101.m2_ref, ...), custom_call_target="tpu_custom_call" | custom-call | flops 4000000000 | bytes 16000000 | tf_op jit(solution)/shard_map/input_grad/pallas_call | solution.py:367
  228.5 1.2 copy-done.6
  229.7 2.6 add_convert_fusion.2
  232.3 1.1 add_parts.2
  233.6 2.3 collective-permute-start.22
  236.1 4.9 %collective-permute-done.21 = bf16[128,768]{1,0:T(8,128)(2,1)S(1)} collective-permute-done((bf16[128,768]{1,0:T(8,128)(2,1)S(1)}, bf16[128,768]{1,0:T(8,128)(2,1)S(1)}, u32[]{:S(2)}, u32[]{:S(2)}) %collective-permute-start.21) | collective-permute-done | bytes 196640 | tf_op jit(solution)/shard_map/ppermute | solution.py:862
  241.0 5.0 %collective-permute-done.22 = bf16[128,768]{1,0:T(8,128)(2,1)S(1)} collective-permute-done((bf16[128,768]{1,0:T(8,128)(2,1)S(1)}, bf16[128,768]{1,0:T(8,128)(2,1)S(1)}, u32[]{:S(2)}, u32[]{:S(2)}) %collective-permute-start.22) | collective-permute-done | bytes 196640 | tf_op jit(solution)/shard_map/ppermute | solution.py:862
  246.0 10.2 %collective-permute-done.23 = bf16[128,768]{1,0:T(8,128)(2,1)S(1)} collective-permute-done((bf16[128,768]{1,0:T(8,128)(2,1)S(1)}, bf16[128,768]{1,0:T(8,128)(2,1)S(1)}, u32[]{:S(2)}, u32[]{:S(2)}) %collective-permute-start.23) | collective-permute-done | bytes 196640 | tf_op jit(solution)/shard_map/ppermute | solution.py:862
  256.9 1.7 pad_maximum_fusion.3
  260.7 19.6 %collective-permute-done.10 = bf16[1792,256]{1,0:T(8,128)(2,1)S(1)} collective-permute-done((bf16[1792,256]{1,0:T(8,128)(2,1)S(1)}, bf16[1792,256]{1,0:T(8,128)(2,1)S(1)}, u32[]{:S(2)}, u32[]{:S(2)}) %collective-permute-start.10) | collective-permute-done | bytes 917536 | tf_op jit(solution)/shard_map/ppermute | solution.py:859
  280.3 1.1 fusion.7
  281.5 2.0 collective-permute-start.11
  283.5 16.9 %collective-permute-done.7 = bf16[512,768]{1,0:T(8,128)(2,1)S(1)} collective-permute-done((bf16[512,768]{1,0:T(8,128)(2,1)}, bf16[512,768]{1,0:T(8,128)(2,1)S(1)}, u32[]{:S(2)}, u32[]{:S(2)}) %collective-permute-start.7) | collective-permute-done | bytes 786464 | tf_op jit(solution)/shard_map/ppermute | solution.py:1050
  301.5 1.4 copy-done.2
  302.8 1.5 add_parts.3
  305.3 1.1 collective-permute-start.13
  307.1 5.2 %collective-permute-done.12 = bf16[224,256]{1,0:T(8,128)(2,1)S(1)} collective-permute-done((bf16[224,256]{1,0:T(8,128)(2,1)S(1)}, bf16[224,256]{1,0:T(8,128)(2,1)S(1)}, u32[]{:S(2)}, u32[]{:S(2)}) %collective-permute-start.12) | collective-permute-done | bytes 114720 | tf_op jit(solution)/shard_map/ppermute | solution.py:862
  312.4 3.8 collective-permute-done.13
  316.1 2.9 collective-permute-done.14
  319.2 1.4 collective-permute-start.16
  320.5 1.3 collective-permute-start.17
  321.8 2.8 collective-permute-done.15
  324.6 3.4 collective-permute-done.16
  328.0 15.3 %collective-permute-done.17 = bf16[224,256]{1,0:T(8,128)(2,1)S(1)} collective-permute-done((bf16[224,256]{1,0:T(8,128)(2,1)S(1)}, bf16[224,256]{1,0:T(8,128)(2,1)S(1)}, u32[]{:S(2)}, u32[]{:S(2)}) %collective-permute-start.17) | collective-permute-done | bytes 114720 | tf_op jit(solution)/shard_map/ppermute | solution.py:862
  344.0 7.2 %collective-permute-done.18 = bf16[896,256]{1,0:T(8,128)(2,1)S(1)} collective-permute-done((bf16[896,256]{1,0:T(8,128)(2,1)S(1)}, bf16[896,256]{1,0:T(8,128)(2,1)S(1)}, u32[]{:S(2)}, u32[]{:S(2)}) %collective-permute-start.18) | collective-permute-done | bytes 458784 | tf_op jit(solution)/shard_map/ppermute | solution.py:859
  351.3 12.9 %collective-permute-done.19 = bf16[1792,256]{1,0:T(8,128)(2,1)S(1)} collective-permute-done((bf16[1792,256]{1,0:T(8,128)(2,1)S(1)}, bf16[1792,256]{1,0:T(8,128)(2,1)S(1)}, u32[]{:S(2)}, u32[]{:S(2)}) %collective-permute-start.19) | collective-permute-done | bytes 917536 | tf_op jit(solution)/shard_map/ppermute | solution.py:859
  364.3 4.4 %collective-permute-start.20 = (bf16[3584,256]{1,0:T(8,128)(2,1)S(1)}, bf16[3584,256]{1,0:T(8,128)(2,1)}, u32[]{:S(2)}, u32[]{:S(2)}) collective-permute-start(bf16[3584,256]{1,0:T(8,128)(2,1)S(1)} %constant_dynamic-update-slice_fusion.5.refs_1_), channel_id=1, source_target_pairs={{0,2},{1,3},{2,0},{3,1},{4,6},{5,7},{6,4},{7,5},{8,10},{9,11},{10,... | collective-permute-start | bytes 5505032 | tf_op jit(solution)/shard_map/ppermute | solution.py:859
  368.8 3.5 collective-permute-done.20.refs_2_
  372.2 5.0 %widen_qkv.1 = (f32[768,2304]{1,0:T(8,128)}, f32[32,256]{1,0:T(8,128)S(1)}) custom-call(s32[4]{0:T(128)S(1)} %pad_add_fusion.refs_0_, bf16[3584,256]{1,0:T(8,128)(2,1)S(1)} %constant_dynamic-update-slice_fusion.5.refs_1_, bf16[3584,256]{1,0:T(8,128)(2,1)} %collective-permute-done.20.refs_2_), custom_call_target="tpu_custom_call" | custom-call | bytes 10780672 | tf_op jit(solution)/shard_map/widen_qkv/pallas_call | solution.py:800
  377.9 12.9 %widen_dense.1 = (f32[3072,768]{1,0:T(8,128)}, f32[768,3072]{1,0:T(8,128)}, f32[768,768]{1,0:T(8,128)}, f32[32,768]{1,0:T(8,128)S(1)}) custom-call(s32[32]{0:T(128)S(1)} %copy-done.3, bf16[7168,768]{1,0:T(8,128)(2,1)} %all-gather.2.cloned.1.call-done.refs_1_), custom_call_target="tpu_custom_call" | custom-call | bytes 33030144 | tf_op jit(solution)/shard_map/widen_dense/pallas_call | solution.py:747
  (110 shorter events, 17.1 us)
Async XLA Ops:
  7.2 2.7 copy-start.15
  7.2 4.0 %copy-start.13 = (bf16[2,768]{1,0:T(2,128)(2,1)S(1)}, bf16[2,768]{1,0:T(2,128)(2,1)}, u32[]{:S(2)}) copy-start(bf16[2,768]{1,0:T(2,128)(2,1)} %param.19) | copy-start | bytes 9220
  7.2 4.6 %copy-start.16 = (bf16[768]{0:T(1024)(128)(2,1)S(1)}, bf16[768]{0:T(1024)(128)(2,1)}, u32[]{:S(2)}) copy-start(bf16[768]{0:T(1024)(128)(2,1)} %param.22) | copy-start | bytes 4612
  7.2 5.2 %copy-start.14 = (bf16[3072]{0:T(1024)(128)(2,1)S(1)}, bf16[3072]{0:T(1024)(128)(2,1)}, u32[]{:S(2)}) copy-start(bf16[3072]{0:T(1024)(128)(2,1)} %param.25) | copy-start | bytes 18436
  7.2 5.8 %copy-start.17 = (bf16[768]{0:T(1024)(128)(2,1)S(1)}, bf16[768]{0:T(1024)(128)(2,1)}, u32[]{:S(2)}) copy-start(bf16[768]{0:T(1024)(128)(2,1)} %param.21) | copy-start | bytes 4612
  7.2 6.4 %copy-start.18 = (bf16[768]{0:T(1024)(128)(2,1)S(1)}, bf16[768]{0:T(1024)(128)(2,1)}, u32[]{:S(2)}) copy-start(bf16[768]{0:T(1024)(128)(2,1)} %param.23) | copy-start | bytes 4612
  7.2 6.9 %copy-start.19 = (bf16[768]{0:T(1024)(128)(2,1)S(1)}, bf16[768]{0:T(1024)(128)(2,1)}, u32[]{:S(2)}) copy-start(bf16[768]{0:T(1024)(128)(2,1)} %param.27) | copy-start | bytes 4612
  7.3 7.5 %copy-start.20 = (bf16[768]{0:T(1024)(128)(2,1)S(1)}, bf16[768]{0:T(1024)(128)(2,1)}, u32[]{:S(2)}) copy-start(bf16[768]{0:T(1024)(128)(2,1)} %param.28) | copy-start | bytes 4612
  7.3 8.1 %copy-start.21 = (bf16[768]{0:T(1024)(128)(2,1)S(1)}, bf16[768]{0:T(1024)(128)(2,1)}, u32[]{:S(2)}) copy-start(bf16[768]{0:T(1024)(128)(2,1)} %param.29) | copy-start | bytes 4612
  7.3 249.6 %reduce-scatter.2.cloned.1.call-start = ((), (), s32[]{:S(2)}) async-start(), calls=%async_computation.1 | async-start | bytes 4866048 | tf_op jit(solution)/shard_map/reduce_scatter | solution.py:1010
  9.7 19.8 %collective-permute-start = (bf16[1,512,768]{2,1,0:T(8,128)(2,1)}, bf16[1,512,768]{2,1,0:T(8,128)(2,1)S(1)}, u32[]{:S(2)}, u32[]{:S(2)}) collective-permute-start(bf16[1,512,768]{2,1,0:T(8,128)(2,1)} %get-tuple-element.142), channel_id=1, source_target_pairs={{0,1},{1,0},{2,3},{3,2},{4,5},{5,4},{6,7},{7,6},{8,9},{9,8},{10,11... | collective-permute-start | bytes 2359304 | tf_op jit(solution)/shard_map/ppermute | solution.py:817
  9.9 18.4 %collective-permute-start.1 = (s32[1,512]{1,0:T(1,128)S(1)}, s32[1,512]{1,0:T(1,128)S(1)}, u32[]{:S(2)}, u32[]{:S(2)}) collective-permute-start(s32[1,512]{1,0:T(1,128)S(1)} %get-tuple-element.160), channel_id=1, source_target_pairs={{0,1},{1,0},{2,3},{3,2},{4,5},{5,4},{6,7},{7,6},{8,9},{9,8},{10,11... | collective-permute-start | bytes 6152 | tf_op jit(solution)/shard_map/ppermute | solution.py:817
  28.4 4.3 %copy-start.7 = (bf16[2,512,768]{2,1,0:T(8,128)(2,1)S(1)}, bf16[2,512,768]{2,1,0:T(8,128)(2,1)}, u32[]{:S(2)}) copy-start(bf16[2,512,768]{2,1,0:T(8,128)(2,1)} %param.30) | copy-start | bytes 4718596
  29.6 1.1 copy-start.8
  32.8 28.3 %collective-permute-start.2 = (bf16[1,512,768]{2,1,0:T(8,128)(2,1)S(1)}, bf16[1,512,768]{2,1,0:T(8,128)(2,1)S(1)}, u32[]{:S(2)}, u32[]{:S(2)}) collective-permute-start(bf16[1,512,768]{2,1,0:T(8,128)(2,1)S(1)} %get-tuple-element.140), channel_id=1, source_target_pairs={{0,1},{1,0},{2,3},{3,2},{4,5},{5,4},{6,7},{7,6},{8,9},{9,8},{10,11... | collective-permute-start | bytes 2359304 | tf_op jit(solution)/shard_map/ppermute | solution.py:817
  100.0 24.5 %collective-permute-start.4 = (f32[32,768]{1,0:T(8,128)}, f32[32,768]{1,0:T(8,128)S(1)}, u32[]{:S(2)}, u32[]{:S(2)}) collective-permute-start(f32[32,768]{1,0:T(8,128)} %get-tuple-element.72), channel_id=1, source_target_pairs={{0,1},{1,0},{2,3},{3,2},{4,5},{5,4},{6,7},{7,6},{8,9},{9,8},{10,11... | collective-permute-start | bytes 294920 | tf_op jit(solution)/shard_map/ppermute | solution.py:1015
  101.3 23.9 %collective-permute-start.3 = (bf16[512,768]{1,0:T(8,128)(2,1)}, bf16[512,768]{1,0:T(8,128)(2,1)S(1)}, u32[]{:S(2)}, u32[]{:S(2)}) collective-permute-start(bf16[512,768]{1,0:T(8,128)(2,1)} %get-tuple-element.71), channel_id=1, source_target_pairs={{0,1},{1,0},{2,3},{3,2},{4,5},{5,4},{6,7},{7,6},{8,9},{9,8},{10,11... | collective-permute-start | bytes 2359304 | tf_op jit(solution)/shard_map/ppermute | solution.py:1013
  101.5 23.0 %copy-start.12 = (f32[32,768]{1,0:T(8,128)S(1)}, f32[32,768]{1,0:T(8,128)}, u32[]{:S(2)}) copy-start(f32[32,768]{1,0:T(8,128)} %get-tuple-element.72) | copy-start | bytes 294916
  101.5 23.7 %copy-start.11 = (bf16[512,768]{1,0:T(8,128)(2,1)S(1)}, bf16[512,768]{1,0:T(8,128)(2,1)}, u32[]{:S(2)}) copy-start(bf16[512,768]{1,0:T(8,128)(2,1)} %get-tuple-element.70) | copy-start | bytes 2359300
  139.8 24.3 %collective-permute-start.5 = (bf16[2048,768]{1,0:T(8,128)(2,1)}, bf16[2048,768]{1,0:T(8,128)(2,1)}, u32[]{:S(2)}, u32[]{:S(2)}) collective-permute-start(bf16[2048,768]{1,0:T(8,128)(2,1)} %get-tuple-element.91.refs_10_), channel_id=1, source_target_pairs={{0,2},{1,3},{2,0},{3,1},{4,6},{5,7},{6,4},{7,5},{8,10},{9,11},{10,... | collective-permute-start | bytes 9437192 | tf_op jit(solution)/shard_map/ppermute | solution.py:859
  142.3 235.6 %all-gather.2.cloned.1.call-start = ((), (), s32[]{:S(2)}) async-start(), calls=%async_computation.2 | async-start | bytes 11354112 | tf_op jit(solution)/shard_map/all_gather | solution.py:1061
  142.3 21.7 %copy-start.5 = (bf16[2048,768]{1,0:T(8,128)(2,1)S(1)}, bf16[2048,768]{1,0:T(8,128)(2,1)}, u32[]{:S(2)}) copy-start(bf16[2048,768]{1,0:T(8,128)(2,1)} %get-tuple-element.93) | copy-start | bytes 9437188
  168.4 23.3 %collective-permute-start.6 = (bf16[1024,768]{1,0:T(8,128)(2,1)}, bf16[1024,768]{1,0:T(8,128)(2,1)S(1)}, u32[]{:S(2)}, u32[]{:S(2)}) collective-permute-start(bf16[1024,768]{1,0:T(8,128)(2,1)} %get-tuple-element.132.refs_10_), channel_id=1, source_target_pairs={{0,4},{1,5},{2,3},{3,2},{4,0},{5,1},{6,7},{7,6},{8,12},{9,13},{10,... | collective-permute-start | bytes 4718600 | tf_op jit(solution)/shard_map/ppermute | solution.py:859
  169.7 22.1 %copy-start.4 = (bf16[1,1024,768]{2,1,0:T(8,128)(2,1)S(1)}, bf16[1,1024,768]{2,1,0:T(8,128)(2,1)}, u32[]{:S(2)}) copy-start(bf16[1,1024,768]{2,1,0:T(8,128)(2,1)} %get-tuple-element.131) | copy-start | bytes 4718596
  193.3 23.4 %copy-start.10 = (bf16[512,768]{1,0:T(8,128)(2,1)S(1)}, bf16[512,768]{1,0:T(8,128)(2,1)}, u32[]{:S(2)}) copy-start(bf16[512,768]{1,0:T(8,128)(2,1)} %get-tuple-element.136.refs_10_) | copy-start | bytes 2359300
  216.4 12.1 %collective-permute-start.9 = (bf16[3584,256]{1,0:T(8,128)(2,1)}, bf16[3584,256]{1,0:T(8,128)(2,1)S(1)}, u32[]{:S(2)}, u32[]{:S(2)}) collective-permute-start(bf16[3584,256]{1,0:T(8,128)(2,1)} %get-tuple-element.106), channel_id=1, source_target_pairs={{0,2},{1,3},{2,0},{3,1},{4,6},{5,7},{6,4},{7,5},{8,10},{9,11},{10,... | collective-permute-start | bytes 5505032 | tf_op jit(solution)/shard_map/ppermute | solution.py:859
  216.7 15.6 %collective-permute-start.8 = (bf16[512,768]{1,0:T(8,128)(2,1)S(1)}, bf16[512,768]{1,0:T(8,128)(2,1)S(1)}, u32[]{:S(2)}, u32[]{:S(2)}) collective-permute-start(bf16[512,768]{1,0:T(8,128)(2,1)S(1)} %copy-done.10), channel_id=1, source_target_pairs={{0,1},{1,0},{2,6},{3,7},{4,5},{5,4},{6,2},{7,3},{8,9},{9,8},{10,14... | collective-permute-start | bytes 2359304 | tf_op jit(solution)/shard_map/ppermute | solution.py:859
  228.5 1.2 copy-start.6
  229.7 2.6 copy-start.1
  233.4 7.6 %collective-permute-start.21 = (bf16[128,768]{1,0:T(8,128)(2,1)S(1)}, bf16[128,768]{1,0:T(8,128)(2,1)S(1)}, u32[]{:S(2)}, u32[]{:S(2)}) collective-permute-start(bf16[128,768]{1,0:T(8,128)(2,1)S(1)} %get-tuple-element.116), channel_id=1, source_target_pairs={{0,8},{2,10},{4,12},{6,14},{8,0},{10,2},{12,4},{14,6},{16,24},{18,... | collective-permute-start | bytes 589832 | tf_op jit(solution)/shard_map/ppermute | solution.py:862
  233.6 12.4 %collective-permute-start.22 = (bf16[128,768]{1,0:T(8,128)(2,1)S(1)}, bf16[128,768]{1,0:T(8,128)(2,1)S(1)}, u32[]{:S(2)}, u32[]{:S(2)}) collective-permute-start(bf16[128,768]{1,0:T(8,128)(2,1)S(1)} %get-tuple-element.117), channel_id=1, source_target_pairs={{0,16},{2,18},{4,20},{6,22},{8,24},{10,26},{12,28},{14,30},{16,0},... | collective-permute-start | bytes 589832 | tf_op jit(solution)/shard_map/ppermute | solution.py:862
  235.9 20.2 %collective-permute-start.23 = (bf16[128,768]{1,0:T(8,128)(2,1)S(1)}, bf16[128,768]{1,0:T(8,128)(2,1)S(1)}, u32[]{:S(2)}, u32[]{:S(2)}) collective-permute-start(bf16[128,768]{1,0:T(8,128)(2,1)S(1)} %get-tuple-element.118), channel_id=1, source_target_pairs={{0,24},{2,26},{4,28},{6,30},{8,16},{10,18},{12,20},{14,22},{16,8},... | collective-permute-start | bytes 589832 | tf_op jit(solution)/shard_map/ppermute | solution.py:862
  258.5 21.8 %collective-permute-start.10 = (bf16[1792,256]{1,0:T(8,128)(2,1)S(1)}, bf16[1792,256]{1,0:T(8,128)(2,1)S(1)}, u32[]{:S(2)}, u32[]{:S(2)}) collective-permute-start(bf16[1792,256]{1,0:T(8,128)(2,1)S(1)} %get-tuple-element.134.refs_0_), channel_id=1, source_target_pairs={{0,4},{1,5},{2,3},{3,2},{4,0},{5,1},{6,7},{7,6},{8,12},{9,13},{10,... | collective-permute-start | bytes 2752520 | tf_op jit(solution)/shard_map/ppermute | solution.py:859
  259.1 41.3 %collective-permute-start.7 = (bf16[512,768]{1,0:T(8,128)(2,1)}, bf16[512,768]{1,0:T(8,128)(2,1)S(1)}, u32[]{:S(2)}, u32[]{:S(2)}) collective-permute-start(bf16[512,768]{1,0:T(8,128)(2,1)} %get-tuple-element.103), channel_id=1, source_target_pairs={{0,1},{1,0},{2,3},{3,2},{4,5},{5,4},{6,7},{7,6},{8,9},{9,8},{10,11... | collective-permute-start | bytes 2359304 | tf_op jit(solution)/shard_map/ppermute | solution.py:1050
  281.5 19.0 %copy-start.9 = (f32[512,768]{1,0:T(8,128)S(1)}, f32[512,768]{1,0:T(8,128)}, u32[]{:S(2)}) copy-start(f32[512,768]{1,0:T(8,128)} %get-tuple-element.102) | copy-start | bytes 4718596
  281.5 20.0 %collective-permute-start.11 = (bf16[896,256]{1,0:T(8,128)(2,1)}, bf16[896,256]{1,0:T(8,128)(2,1)}, u32[]{:S(2)}, u32[]{:S(2)}) collective-permute-start(bf16[896,256]{1,0:T(8,128)(2,1)} %get-tuple-element.137), channel_id=1, source_target_pairs={{0,1},{1,0},{2,6},{3,7},{4,5},{5,4},{6,2},{7,3},{8,9},{9,8},{10,14... | collective-permute-start | bytes 1376264 | tf_op jit(solution)/shard_map/ppermute | solution.py:859
  300.7 3.7 copy-start
  301.5 1.4 copy-start.2
  304.4 7.9 %collective-permute-start.12 = (bf16[224,256]{1,0:T(8,128)(2,1)S(1)}, bf16[224,256]{1,0:T(8,128)(2,1)S(1)}, u32[]{:S(2)}, u32[]{:S(2)}) collective-permute-start(bf16[224,256]{1,0:T(8,128)(2,1)S(1)} %get-tuple-element.109), channel_id=1, source_target_pairs={{0,8},{2,10},{4,12},{6,14},{8,0},{10,2},{12,4},{14,6},{16,24},{18,... | collective-permute-start | bytes 344072 | tf_op jit(solution)/shard_map/ppermute | solution.py:862
  305.3 10.8 %collective-permute-start.13 = (bf16[224,256]{1,0:T(8,128)(2,1)S(1)}, bf16[224,256]{1,0:T(8,128)(2,1)S(1)}, u32[]{:S(2)}, u32[]{:S(2)}) collective-permute-start(bf16[224,256]{1,0:T(8,128)(2,1)S(1)} %get-tuple-element.110), channel_id=1, source_target_pairs={{0,16},{2,18},{4,20},{6,22},{8,24},{10,26},{12,28},{14,30},{16,0},... | collective-permute-start | bytes 344072 | tf_op jit(solution)/shard_map/ppermute | solution.py:862
  306.5 12.6 %collective-permute-start.14 = (bf16[224,256]{1,0:T(8,128)(2,1)S(1)}, bf16[224,256]{1,0:T(8,128)(2,1)S(1)}, u32[]{:S(2)}, u32[]{:S(2)}) collective-permute-start(bf16[224,256]{1,0:T(8,128)(2,1)S(1)} %get-tuple-element.111), channel_id=1, source_target_pairs={{0,24},{2,26},{4,28},{6,30},{8,16},{10,18},{12,20},{14,22},{16,8},... | collective-permute-start | bytes 344072 | tf_op jit(solution)/shard_map/ppermute | solution.py:862
  319.1 5.5 %collective-permute-start.15 = (bf16[224,256]{1,0:T(8,128)(2,1)S(1)}, bf16[224,256]{1,0:T(8,128)(2,1)S(1)}, u32[]{:S(2)}, u32[]{:S(2)}) collective-permute-start(bf16[224,256]{1,0:T(8,128)(2,1)S(1)} %get-tuple-element.130), channel_id=1, source_target_pairs={{0,8},{2,10},{4,12},{6,14},{8,0},{10,2},{12,4},{14,6},{16,24},{18,... | collective-permute-start | bytes 344072 | tf_op jit(solution)/shard_map/ppermute | solution.py:862
  319.2 8.8 %collective-permute-start.16 = (bf16[224,256]{1,0:T(8,128)(2,1)S(1)}, bf16[224,256]{1,0:T(8,128)(2,1)S(1)}, u32[]{:S(2)}, u32[]{:S(2)}) collective-permute-start(bf16[224,256]{1,0:T(8,128)(2,1)S(1)} %get-tuple-element.130), channel_id=1, source_target_pairs={{0,16},{2,18},{4,20},{6,22},{8,24},{10,26},{12,28},{14,30},{16,0},... | collective-permute-start | bytes 344072 | tf_op jit(solution)/shard_map/ppermute | solution.py:862
  320.5 22.8 %collective-permute-start.17 = (bf16[224,256]{1,0:T(8,128)(2,1)S(1)}, bf16[224,256]{1,0:T(8,128)(2,1)S(1)}, u32[]{:S(2)}, u32[]{:S(2)}) collective-permute-start(bf16[224,256]{1,0:T(8,128)(2,1)S(1)} %get-tuple-element.130), channel_id=1, source_target_pairs={{0,24},{2,26},{4,28},{6,30},{8,16},{10,18},{12,20},{14,22},{16,8},... | collective-permute-start | bytes 344072 | tf_op jit(solution)/shard_map/ppermute | solution.py:862
  343.4 7.8 %collective-permute-start.18 = (bf16[896,256]{1,0:T(8,128)(2,1)S(1)}, bf16[896,256]{1,0:T(8,128)(2,1)S(1)}, u32[]{:S(2)}, u32[]{:S(2)}) collective-permute-start(bf16[896,256]{1,0:T(8,128)(2,1)S(1)} %pad_maximum_fusion.2), channel_id=1, source_target_pairs={{0,1},{1,0},{2,6},{3,7},{4,5},{5,4},{6,2},{7,3},{8,9},{9,8},{10,14... | collective-permute-start | bytes 1376264 | tf_op jit(solution)/shard_map/ppermute | solution.py:859
  351.3 12.9 %collective-permute-start.19 = (bf16[1792,256]{1,0:T(8,128)(2,1)S(1)}, bf16[1792,256]{1,0:T(8,128)(2,1)S(1)}, u32[]{:S(2)}, u32[]{:S(2)}) collective-permute-start(bf16[1792,256]{1,0:T(8,128)(2,1)S(1)} %get-tuple-element.143), channel_id=1, source_target_pairs={{0,4},{1,5},{2,3},{3,2},{4,0},{5,1},{6,7},{7,6},{8,12},{9,13},{10,... | collective-permute-start | bytes 2752520 | tf_op jit(solution)/shard_map/ppermute | solution.py:859
  364.3 8.0 %collective-permute-start.20 = (bf16[3584,256]{1,0:T(8,128)(2,1)S(1)}, bf16[3584,256]{1,0:T(8,128)(2,1)}, u32[]{:S(2)}, u32[]{:S(2)}) collective-permute-start(bf16[3584,256]{1,0:T(8,128)(2,1)S(1)} %constant_dynamic-update-slice_fusion.5.refs_1_), channel_id=1, source_target_pairs={{0,2},{1,3},{2,0},{3,1},{4,6},{5,7},{6,4},{7,5},{8,10},{9,11},{10,... | collective-permute-start | bytes 5505032 | tf_op jit(solution)/shard_map/ppermute | solution.py:859
  368.8 9.1 %copy-start.3 = (s32[32]{0:T(128)S(1)}, s32[32]{0:T(128)}, u32[]{:S(2)}) copy-start(s32[32]{0:T(128)} %constant.91.clone.refs_0_) | copy-start | bytes 388
Sparse Core Ops, SparseCore 0:
  142.4 114.4 reduce-scatter.1
  260.8 102.2 all-gather.1
